TPU v7x, 32 devices: a whole 2x2x4 slice. The times are simulated.
32 devices in a mesh: ty: 4 (over z), tx: 8 (over y, x, core).
Axes of the slice: x: 2, y: 2, z: 4, core: 2. Of those that a mesh axis runs over, the one named last changes fastest.
Arguments:
- specimen: float32 [2, 4096, 4096], P(None, 'ty', 'tx'), may hold values from -6 to 6
- probe_modes: float32 [2, 3, 512, 512], replicated, may hold values from -6 to 6
- amplitude: float32 [64, 512, 512], P(('ty', 'tx')), may hold values from 0.5 to 3
- offsets: int32 [64, 2], P(('ty', 'tx')), may hold values from 0 to 1023, as said below
- live_slots: int32 [64], P(('ty', 'tx')), may hold values from 0 to 1, as said below
Outputs:
- specimen_grad: float32 [2, 4096, 4096], P(None, 'ty', 'tx')
- probe_grad: float32 [2, 3, 512, 512], replicated
Inputs may be any that keep to these rules, and one draw needn't show every extreme that they name: `offsets`: offsets are a row below 1024 and a column below 512 within the tile of the slot's device, chosen so that the 512 x 512 patch lies inside the object. `live_slots`: on each device the live slots come first; the two devices with tx indices 2m and 2m+1 and the same ty index hold exactly 2 live slots together.
All inputs are finite; a program needn't handle non-finite values.
Results may differ from a plain program's by a relative error of at most 0.0038.
The roundings to bfloat16 on the way count: a program that leaves them out, or rounds other values in their place, can miss the bound.
Values sent between devices are 32-bit elements; how exact they have to be, the bound alone decides.
A program may use at most 128 MiB of HBM per device.

v0:
```python
import math

import jax
import jax.numpy as jnp
from jax import lax
from jax.sharding import PartitionSpec as P


def passed_along(value, axis, steps):
    count = lax.axis_size(axis)
    initial, last = (max(0, -steps), min(count, count - steps))
    return lax.ppermute(value, axis, [(source, source + steps) for source in range(initial, last)])


def partner(value, axis, apart):
    mask = 2**apart
    pairs = [(source, source ^ mask) for source in range(lax.axis_size(axis))]
    return lax.ppermute(value, axis, pairs)


def tables(length):
    index = jnp.arange(length, dtype=jnp.int32)
    phase = index[:, None] * index[None, :] % length
    angle = phase.astype(jnp.float32) * (2.0 * math.pi / length)
    scale = 1.0 / math.sqrt(length)
    return (
        (jnp.cos(angle) * scale).astype(jnp.bfloat16),
        (jnp.sin(angle) * scale).astype(jnp.bfloat16),
    )


def transform(real_part, imag_part, cos_table, sin_table, orient):
    length = real_part.shape[-1]
    stacked = jnp.concatenate([real_part, imag_part], axis=2)
    cos_part = jnp.einsum("ij,mjk->mik", cos_table, stacked, preferred_element_type=jnp.float32)
    sin_part = jnp.einsum("ij,mjk->mik", sin_table, stacked, preferred_element_type=jnp.float32)
    middle_re = (cos_part[:, :, :length] + orient * sin_part[:, :, length:]).astype(jnp.bfloat16)
    middle_im = (cos_part[:, :, length:] - orient * sin_part[:, :, :length]).astype(jnp.bfloat16)
    stacked = jnp.concatenate([middle_re, middle_im], axis=1)
    cos_part = jnp.einsum("mij,jk->mik", stacked, cos_table, preferred_element_type=jnp.float32)
    sin_part = jnp.einsum("mij,jk->mik", stacked, sin_table, preferred_element_type=jnp.float32)
    result_re = cos_part[:, :length] + orient * sin_part[:, length:]
    result_im = cos_part[:, length:] - orient * sin_part[:, :length]
    return (result_re, result_im)


def slot_terms(window, probe_modes, measured, alive_mask, cos_table, sin_table):
    window_re, window_im = (window[0], window[1])
    probe_re, probe_im = (probe_modes[0], probe_modes[1])
    wave_re = (probe_re * window_re - probe_im * window_im).astype(jnp.bfloat16)
    wave_im = (probe_re * window_im + probe_im * window_re).astype(jnp.bfloat16)
    far_re, far_im = transform(wave_re, wave_im, cos_table, sin_table, 1.0)
    intensity = jnp.sum(far_re * far_re + far_im * far_im, axis=0)
    factor = measured * lax.rsqrt(jnp.maximum(intensity, 1.0)) - 1.0
    delta_re = (far_re * factor).astype(jnp.bfloat16)
    delta_im = (far_im * factor).astype(jnp.bfloat16)
    back_re, back_im = transform(delta_re, delta_im, cos_table, sin_table, -1.0)
    back_re = back_re * alive_mask
    back_im = back_im * alive_mask
    grad_re = jnp.sum(probe_re * back_re + probe_im * back_im, axis=0)
    grad_im = jnp.sum(probe_re * back_im - probe_im * back_re, axis=0)
    mode_re = window_re * back_re + window_im * back_im
    mode_im = window_re * back_im - window_im * back_re
    return (jnp.stack([grad_re, grad_im]), jnp.stack([mode_re, mode_im]))


def local(specimen, probe_modes, amplitude, offsets, live_slots):
    tile_h = specimen.shape[1]
    tile_w = specimen.shape[2]
    width = probe_modes.shape[2]
    slots = live_slots.shape[0]
    tile_cols = lax.axis_size("tx")
    devices_all = lax.axis_size("ty") * lax.axis_size("tx")
    anchor = jnp.zeros((), jnp.int32)
    right_part = passed_along(specimen, "tx", -1)
    lower_part = passed_along(specimen[:, :width, :], "ty", -1)
    corner_part = passed_along(specimen[:, :width, :width], ("ty", "tx"), -(tile_cols + 1))
    upper_rows = jnp.concatenate([specimen, right_part], axis=2)
    lower_rows = jnp.concatenate([lower_part, corner_part], axis=2)
    extended = jnp.concatenate([upper_rows, lower_rows], axis=1)
    cos_table, sin_table = tables(width)

    def crop(row_at, col_at):
        return lax.dynamic_slice(extended, (anchor, row_at, col_at), (2, width, width))

    windows = jax.vmap(crop)(offsets[:, 0], offsets[:, 1])
    alive_own = live_slots.astype(jnp.float32)

    def process(slot_items):
        window, measured, alive_mask = slot_items
        return slot_terms(window, probe_modes, measured, alive_mask, cos_table, sin_table)

    half_slots = slots // 2
    live_count = jnp.sum(alive_own)
    got_windows, got_measured, got_count = partner(
        (windows[half_slots:], amplitude[half_slots:], live_count), "tx", 0
    )
    position = jnp.arange(half_slots, dtype=jnp.int32)
    taken = jnp.minimum(live_count, float(half_slots)).astype(jnp.int32)
    got_alive = ((position + half_slots).astype(jnp.float32) < got_count).astype(jnp.float32)
    pool_windows = jnp.concatenate([windows[:half_slots], got_windows], axis=0)
    pool_measured = jnp.concatenate([amplitude[:half_slots], got_measured], axis=0)
    pool_alive = jnp.concatenate([alive_own[:half_slots], got_alive], axis=0)
    order_index = jnp.where(position < taken, position, half_slots + position - taken)
    work_windows = jnp.take(pool_windows, order_index, axis=0)
    work_measured = jnp.take(pool_measured, order_index, axis=0)
    work_alive = jnp.take(pool_alive, order_index, axis=0)
    grad_terms, probe_terms = lax.map(process, (work_windows, work_measured, work_alive))
    padded_terms = jnp.concatenate([grad_terms, jnp.zeros_like(grad_terms)], axis=0)
    returned = jnp.take(padded_terms, taken + position, axis=0)
    got_back = partner(returned, "tx", 0)
    kept = jnp.where((position < taken)[:, None, None, None], grad_terms, 0.0)
    own_terms = jnp.concatenate([kept, got_back], axis=0)
    probe_total = lax.psum(jnp.sum(probe_terms, axis=0), ("ty", "tx"))
    probe_grad = probe_total * (1.0 / math.sqrt(slots * devices_all))

    def place(slot_index, grad_ext):
        row_at = offsets[slot_index, 0]
        col_at = offsets[slot_index, 1]
        current = lax.dynamic_slice(grad_ext, (anchor, row_at, col_at), (2, width, width))
        return lax.dynamic_update_slice(
            grad_ext, current + own_terms[slot_index], (anchor, row_at, col_at)
        )

    grad_ext = lax.fori_loop(0, slots, place, jnp.zeros(extended.shape, jnp.float32))
    from_left = passed_along(grad_ext[:, :tile_h, tile_w:], "tx", 1)
    from_above = passed_along(grad_ext[:, tile_h:, :tile_w], "ty", 1)
    from_diagonal = passed_along(grad_ext[:, tile_h:, tile_w:], ("ty", "tx"), tile_cols + 1)
    core_grad = grad_ext[:, :tile_h, :tile_w]
    core_grad = core_grad.at[:, :, :width].add(from_left)
    core_grad = core_grad.at[:, :width, :].add(from_above)
    core_grad = core_grad.at[:, :width, :width].add(from_diagonal)
    return (core_grad, probe_grad)


def solution(mesh):
    return jax.shard_map(
        local,
        mesh=mesh,
        in_specs=(
            P(None, "ty", "tx"),
            P(),
            P(("ty", "tx"), None, None),
            P(("ty", "tx"), None),
            P(("ty", "tx")),
        ),
        out_specs=(P(None, "ty", "tx"), P()),
        check_vma=False,
    )
```

profile of v0, /device:TPU:27, one launch (start us, length us, event | category | flops | bytes accessed | tf_op | source)
XLA Modules:
  0.0 532.9 jit_solution(7659781623877569261)
XLA Ops:
  15.0 3.3 collective-permute-start.1
  18.4 41.6 %collective-permute-done.2 = f32[2,512,512]{2,1,0:T(8,128)S(1)} collective-permute-done((f32[2,512,512]{2,1,0:T(8,128)}, f32[2,512,512]{2,1,0:T(8,128)S(1)}, u32[]{:S(2)}, u32[]{:S(2)}) %collective-permute-start.2) | collective-permute-done | bytes 2097184 | tf_op jit(solution)/shard_map/ppermute | solution.py:12
  60.0 44.9 %collective-permute-done.1 = f32[2,512,512]{2,1,0:T(8,128)} collective-permute-done((f32[2,512,512]{2,1,0:T(8,128)}, f32[2,512,512]{2,1,0:T(8,128)}, u32[]{:S(2)}, u32[]{:S(2)}) %collective-permute-start.1) | collective-permute-done | bytes 2097184 | tf_op jit(solution)/shard_map/ppermute | solution.py:12
  105.0 10.5 %maximum_maximum_fusion = f32[2,1536,1024]{2,1,0:T(8,128)} fusion(f32[2,512,512]{2,1,0:T(8,128)S(1)} %collective-permute-done.2, f32[2,512,512]{2,1,0:T(8,128)} %collective-permute-done.1, f32[2,1024,512]{2,1,0:T(8,128)} %collective-permute-done, f32[2,1024,512]{2,1,0:T(8,128)} %param.17), kind=kLoop, calls=%fused_computation.5 | loop fusion | flops 9437184 | bytes 25165824 | tf_op jit(solution)/shard_map/concatenate | solution.py:80
  115.5 11.5 %while.27 = (s32[]{:T(128)}, f32[2,1536,1024]{2,1,0:T(8,128)}, s32[2,3]{1,0:T(2,128)S(1)}, f32[2,2,512,512]{3,2,1,0:T(8,128)}, s32[]{:T(128)}) while((s32[]{:T(128)}, f32[2,1536,1024]{2,1,0:T(8,128)}, s32[2,3]{1,0:T(2,128)S(1)}, f32[2,2,512,512]{3,2,1,0:T(8,128)}, s32[]{:T(128)}) %tuple.95), condition=%wide.while_cond.4, body=%wide.while_body.4.sunk | while | flops 2 | bytes 4195445 | solution.py:84
  116.1 5.0 bitcast_dynamic-update-slice_fusion.2
  121.7 5.0 bitcast_dynamic-update-slice_fusion.2
  127.0 4.8 fusion.99
  144.9 5.4 %convolution_bitcast_fusion.1 = f32[3,512,1024]{2,1,0:T(8,128)S(1)} fusion(bf16[3,512,512]{2,1,0:T(8,128)(2,1)S(1)} %get-tuple-element.229, bf16[3,512,512]{2,1,0:T(8,128)(2,1)S(1)} %get-tuple-element.228), kind=kOutput, calls=%fused_computation.57 | convolution fusion | flops 1621098496 | bytes 9437184 | tf_op jit(solution)/shard_map/while/body/eval_jaxpr/ij,mjk->mik/dot_general | solution.py:35
  150.4 8.7 %convolution_bitcast_fusion = f32[3,512,1024]{2,1,0:T(8,128)} fusion(bf16[3,512,512]{2,1,0:T(8,128)(2,1)S(1)} %get-tuple-element.229, bf16[3,512,512]{2,1,0:T(8,128)(2,1)S(1)} %get-tuple-element.228), kind=kOutput, calls=%fused_computation.56 | convolution fusion | flops 1621098496 | bytes 9437184 | tf_op jit(solution)/shard_map/while/body/eval_jaxpr/ij,mjk->mik/dot_general | solution.py:36
  159.0 4.2 fusion.9
  163.2 5.5 %fusion.23 = f32[3,1024,512]{1,2,0:T(8,128)S(1)} fusion(bf16[3,512,512]{2,1,0:T(8,128)(2,1)S(1)} %get-tuple-element.227, bf16[3,512,512]{2,1,0:T(8,128)(2,1)S(1)} %get-tuple-element.226), kind=kOutput, calls=%fused_computation.71 | convolution fusion | flops 1621098496 | bytes 9437184 | tf_op jit(solution)/shard_map/while/body/eval_jaxpr/mij,jk->mik/dot_general | solution.py:41
  168.7 5.6 %fusion.24 = f32[3,1024,512]{1,2,0:T(8,128)S(1)} fusion(bf16[3,512,512]{2,1,0:T(8,128)(2,1)S(1)} %get-tuple-element.227, bf16[3,512,512]{2,1,0:T(8,128)(2,1)S(1)} %get-tuple-element.226), kind=kOutput, calls=%fused_computation.72 | convolution fusion | flops 1621098496 | bytes 9437184 | tf_op jit(solution)/shard_map/while/body/eval_jaxpr/mij,jk->mik/dot_general | solution.py:40
  177.4 5.8 %multiply_convert_fusion.1 = (bf16[3,512,512]{1,2,0:T(8,128)(2,1)S(1)}, bf16[3,512,512]{1,2,0:T(8,128)(2,1)}) fusion(f32[512,512]{0,1:T(8,128)S(1)} %fusion.32, f32[3,1024,512]{1,2,0:T(8,128)S(1)} %fusion.23, f32[3,1024,512]{1,2,0:T(8,128)} %copy-done), kind=kLoop, calls=%fused_computation.54 | loop fusion | flops 4718592 | bytes 16777216 | tf_op jit(solution)/shard_map/while/body/eval_jaxpr/convert_element_type | solution.py:55
  183.2 7.0 %convolution_bitcast_fusion.2 = f32[3,512,1024]{2,1,0:T(8,128)S(1)} fusion(bf16[3,512,512]{1,2,0:T(8,128)(2,1)} %get-tuple-element.221, bf16[3,512,512]{1,2,0:T(8,128)(2,1)S(1)} %get-tuple-element.220), kind=kOutput, calls=%fused_computation.58 | convolution fusion | flops 1621098496 | bytes 9437184 | tf_op jit(solution)/shard_map/while/body/eval_jaxpr/ij,mjk->mik/dot_general | solution.py:36
  190.2 8.3 %convolution_bitcast_fusion.3 = f32[3,512,1024]{2,1,0:T(8,128)} fusion(bf16[3,512,512]{1,2,0:T(8,128)(2,1)S(1)} %copy-done.6, bf16[3,512,512]{1,2,0:T(8,128)(2,1)S(1)} %get-tuple-element.220), kind=kOutput, calls=%fused_computation.59 | convolution fusion | flops 1621098496 | bytes 9437184 | tf_op jit(solution)/shard_map/while/body/eval_jaxpr/ij,mjk->mik/dot_general | solution.py:35
  198.5 4.5 fusion.7
  203.1 5.1 fusion.21
  208.2 5.5 %fusion.22 = f32[3,1024,512]{2,1,0:T(8,128)S(1)} fusion(bf16[3,512,512]{2,1,0:T(8,128)(2,1)S(1)} %get-tuple-element.225, bf16[3,512,512]{2,1,0:T(8,128)(2,1)S(1)} %get-tuple-element.224), kind=kOutput, calls=%fused_computation.70 | convolution fusion | flops 1621098496 | bytes 9437184 | tf_op jit(solution)/shard_map/while/body/eval_jaxpr/mij,jk->mik/dot_general | solution.py:40
  216.8 3.4 fusion.15
  225.4 4.2 pad_maximum_fusion.1
  229.7 6.1 %broadcast_in_dim.55 = f32[2,1536,1024]{2,1,0:T(8,128)} broadcast(f32[]{:T(128)} %constant.198.clone.1), dimensions={} | broadcast | bytes 12582916 | tf_op jit(solution)/shard_map/broadcast_in_dim | solution.py:125
  235.8 43.8 %while.26 = (s32[]{:T(128)}, f32[2,1536,1024]{2,1,0:T(8,128)}, s32[2,2]{1,0:T(2,128)S(1)}, f32[2,2,512,512]{3,2,1,0:T(8,128)}, s32[]{:T(128)}, /*index=5*/s32[]{:T(128)}, s32[]{:T(128)}, s32[]{:T(128)}) while((s32[]{:T(128)}, f32[2,1536,1024]{2,1,0:T(8,128)}, s32[2,2]{1,0:T(2,128)S(1)}, f32[2,2,512,512]{3,2,1,0:T(8,128)}, s32[]{:T(128)}, ...), condition=%wide.region_5.7_spmd, body=%wide.region_4.6_spmd.sunk | while | flops 524296 | bytes 10485957 | solution.py:125
  243.4 14.1 %dynamic_update_slice.14 = f32[2,1536,1024]{2,1,0:T(8,128)} dynamic-update-slice(f32[2,1536,1024]{2,1,0:T(8,128)} %get-tuple-element.321, f32[2,512,512]{2,1,0:T(8,128)S(1)} %bitcast_add_fusion.2, s32[]{:T(128)} %constant.197.clone.1..sunk, s32[]{:T(128)S(6)} %select_n.152, s32[]{:T(128)S(6)} %select_n.153) | dynamic-update-slice | bytes 4194308 | tf_op jit(solution)/shard_map/while/body/eval_jaxpr/dynamic_update_slice | solution.py:121
  265.1 14.4 %dynamic_update_slice.14 = f32[2,1536,1024]{2,1,0:T(8,128)} dynamic-update-slice(f32[2,1536,1024]{2,1,0:T(8,128)} %get-tuple-element.321, f32[2,512,512]{2,1,0:T(8,128)S(1)} %bitcast_add_fusion.2, s32[]{:T(128)} %constant.197.clone.1..sunk, s32[]{:T(128)S(6)} %select_n.152, s32[]{:T(128)S(6)} %select_n.153) | dynamic-update-slice | bytes 4194308 | tf_op jit(solution)/shard_map/while/body/eval_jaxpr/dynamic_update_slice | solution.py:121
  279.6 4.8 slice.213
  284.4 5.2 collective-permute-start.7
  289.6 3.4 pad_maximum_fusion
  293.1 4.8 fusion.98
  300.6 208.4 %all-reduce.3.cloned.1.call-done = f32[2,3,512,512]{3,2,1,0:T(8,128)} async-done(((f32[2,3,512,512]{3,2,1,0:T(8,128)}), f32[2,3,512,512]{3,2,1,0:T(8,128)}) %all-reduce.3.cloned.1.call-update) | async-done | bytes 6291472 | tf_op jit(solution)/shard_map/psum | solution.py:114
  509.0 6.8 %broadcast_multiply_fusion = f32[2,3,512,512]{3,2,1,0:T(8,128)} fusion(f32[2,3,512,512]{3,2,1,0:T(8,128)} %all-reduce.3.cloned.1.call-done), kind=kLoop, calls=%fused_computation.50 | loop fusion | flops 1572864 | bytes 12582912 | tf_op jit(solution)/shard_map/mul | solution.py:115
  515.9 4.5 slice_add_fusion
  (73 shorter events, 47.1 us)
Async XLA Ops:
  7.2 11.1 %copy-start.7 = (s32[2,2]{1,0:T(2,128)S(1)}, s32[2,2]{1,0:T(2,128)}, u32[]{:S(2)}) copy-start(s32[2,2]{1,0:T(2,128)} %param.20) | copy-start | bytes 52
  7.2 501.9 %all-reduce.3.cloned.1.call-start = ((), (), s32[]{:S(2)}) async-start(), calls=%async_computation | async-start | bytes 12582912 | tf_op jit(solution)/shard_map/psum | solution.py:114
  7.2 97.8 %collective-permute-start = (f32[2,1024,512]{2,1,0:T(8,128)}, f32[2,1024,512]{2,1,0:T(8,128)}, u32[]{:S(2)}, u32[]{:S(2)}) collective-permute-start(f32[2,1024,512]{2,1,0:T(8,128)} %param.17), channel_id=1, source_target_pairs={{1,0},{2,1},{3,2},{4,3},{5,4},{6,5},{7,6},{9,8},{10,9},{11,10},{12... | collective-permute-start | bytes 12582920 | tf_op jit(solution)/shard_map/ppermute | solution.py:12
  12.9 47.1 %collective-permute-start.2 = (f32[2,512,512]{2,1,0:T(8,128)}, f32[2,512,512]{2,1,0:T(8,128)S(1)}, u32[]{:S(2)}, u32[]{:S(2)}) collective-permute-start(f32[2,512,512]{2,1,0:T(8,128)} %slice.185), channel_id=1, source_target_pairs={{9,0},{10,1},{11,2},{12,3},{13,4},{14,5},{15,6},{16,7},{17,8},{18,... | collective-permute-start | bytes 6291464 | tf_op jit(solution)/shard_map/ppermute | solution.py:12
  15.0 90.0 %collective-permute-start.1 = (f32[2,512,512]{2,1,0:T(8,128)}, f32[2,512,512]{2,1,0:T(8,128)}, u32[]{:S(2)}, u32[]{:S(2)}) collective-permute-start(f32[2,512,512]{2,1,0:T(8,128)} %slice.185), channel_id=1, source_target_pairs={{8,0},{16,8},{24,16},{9,1},{17,9},{25,17},{10,2},{18,10},{26,18},{... | collective-permute-start | bytes 6291464 | tf_op jit(solution)/shard_map/ppermute | solution.py:12
  127.0 5.8 %copy-start.8 = (s32[2]{0:T(128)S(1)}, s32[2]{0:T(128)}, u32[]{:S(2)}) copy-start(s32[2]{0:T(128)} %param.21) | copy-start | bytes 28
  127.0 6.5 %copy-start.5 = (f32[2,512,512]{2,1,0:T(8,128)S(1)}, f32[2,512,512]{2,1,0:T(8,128)}, u32[]{:S(2)}) copy-start(f32[2,512,512]{2,1,0:T(8,128)} %param.19) | copy-start | bytes 6291460
  131.8 9.0 %collective-permute-start.3 = (f32[1,2,512,512]{3,2,1,0:T(8,128)}, f32[1,2,512,512]{3,2,1,0:T(8,128)}, u32[]{:S(2)}, u32[]{:S(2)}) collective-permute-start(f32[1,2,512,512]{3,2,1,0:T(8,128)} %get-tuple-element.231), channel_id=1, source_target_pairs={{0,1},{1,0},{2,3},{3,2},{4,5},{5,4},{6,7},{7,6},{8,9},{9,8},{10,11... | collective-permute-start | bytes 6291464 | tf_op jit(solution)/shard_map/ppermute | solution.py:18
  133.4 5.4 %collective-permute-start.5 = (f32[]{:T(128)}, f32[]{:T(128)}, u32[]{:S(2)}, u32[]{:S(2)}) collective-permute-start(f32[]{:T(128)} %convert_reduce_fusion), channel_id=1, source_target_pairs={{0,1},{1,0},{2,3},{3,2},{4,5},{5,4},{6,7},{7,6},{8,9},{9,8},{10,11... | collective-permute-start | bytes 20 | tf_op jit(solution)/shard_map/ppermute | solution.py:18
  135.9 41.1 %collective-permute-start.4 = (f32[1,512,512]{1,2,0:T(8,128)}, f32[1,512,512]{1,2,0:T(8,128)}, u32[]{:S(2)}, u32[]{:S(2)}) collective-permute-start(f32[1,512,512]{1,2,0:T(8,128)} %copy.25), channel_id=1, source_target_pairs={{0,1},{1,0},{2,3},{3,2},{4,5},{5,4},{6,7},{7,6},{8,9},{9,8},{10,11... | collective-permute-start | bytes 3145736 | tf_op jit(solution)/shard_map/ppermute | solution.py:18
  137.1 6.3 %slice-start = ((s8[6291456]{0:T(1024)(128)(4,1)}), s8[2097152]{0:T(1024)(128)(4,1)S(1)}, s32[]{:S(2)}) async-start(s8[6291456]{0:T(1024)(128)(4,1)} %bitcast.107), calls=%async_computation.1 | async-start | bytes 4194304
  140.9 2.8 slice-start.1
  174.3 2.7 copy-start
  183.2 7.0 %copy-start.6 = (bf16[3,512,512]{1,2,0:T(8,128)(2,1)S(1)}, bf16[3,512,512]{1,2,0:T(8,128)(2,1)}, u32[]{:S(2)}) copy-start(bf16[3,512,512]{1,2,0:T(8,128)(2,1)} %get-tuple-element.221) | copy-start | bytes 4718596
  220.2 1.0 copy-start.4
  221.1 4.3 collective-permute-start.6
  279.6 10.0 %copy-start.1 = (f32[1,3,512,512]{3,2,1,0:T(8,128)S(1)}, f32[1,3,512,512]{3,2,1,0:T(8,128)}, u32[]{:S(2)}) copy-start(f32[1,3,512,512]{3,2,1,0:T(8,128)} %get-tuple-element.230) | copy-start | bytes 9437188
  279.6 10.0 %copy-start.2 = (f32[1,3,512,512]{3,2,1,0:T(8,128)S(1)}, f32[1,3,512,512]{3,2,1,0:T(8,128)}, u32[]{:S(2)}) copy-start(f32[1,3,512,512]{3,2,1,0:T(8,128)} %get-tuple-element.213) | copy-start | bytes 9437188
  284.4 231.4 %collective-permute-start.7 = (f32[2,1024,512]{2,1,0:T(8,128)}, f32[2,1024,512]{2,1,0:T(8,128)}, u32[]{:S(2)}, u32[]{:S(2)}) collective-permute-start(f32[2,1024,512]{2,1,0:T(8,128)} %slice.213), channel_id=1, source_target_pairs={{0,1},{1,2},{2,3},{3,4},{4,5},{5,6},{6,7},{8,9},{9,10},{10,11},{11... | collective-permute-start | bytes 12582920 | tf_op jit(solution)/shard_map/ppermute | solution.py:12
  297.8 223.0 %collective-permute-start.8 = (f32[2,512,512]{2,1,0:T(8,128)}, f32[2,512,512]{2,1,0:T(8,128)S(1)}, u32[]{:S(2)}, u32[]{:S(2)}) collective-permute-start(f32[2,512,512]{2,1,0:T(8,128)} %get-tuple-element.223), channel_id=1, source_target_pairs={{0,8},{8,16},{16,24},{1,9},{9,17},{17,25},{2,10},{10,18},{18,26},{... | collective-permute-start | bytes 6291464 | tf_op jit(solution)/shard_map/ppermute | solution.py:12
  299.1 222.3 %collective-permute-start.9 = (f32[2,512,512]{2,1,0:T(8,128)}, f32[2,512,512]{2,1,0:T(8,128)}, u32[]{:S(2)}, u32[]{:S(2)}) collective-permute-start(f32[2,512,512]{2,1,0:T(8,128)} %get-tuple-element.222), channel_id=1, source_target_pairs={{0,9},{1,10},{2,11},{3,12},{4,13},{5,14},{6,15},{7,16},{8,17},{9,1... | collective-permute-start | bytes 6291464 | tf_op jit(solution)/shard_map/ppermute | solution.py:12
  523.8 2.0 copy-start.3
Sparse Core Ops, SparseCore 0:
  293.2 215.7 all-reduce.2
where the time goes:
time: 541 us; the launch traced here: 533 us
  waiting for transfers between devices  298 us (55%)
  local copies, waits for them, and re-layouts  73.9 us (14%)
  other arithmetic  67.9 us (13%)
  matrix products  51.1 us (9%)
  starting transfers between devices  17.4 us (3%)
  between operations  16.5 us (3%)
  loops' own time  8.19 us (2%)
    psum x1, waiting for transfers between devices, local(): probe_total = lax.psum(jnp.sum(probe_terms, axis=0), ('ty', 'tx'))  208 us
    ppermute x6, waiting for transfers between devices, passed_along(): lax.ppermute(value, axis, [(source, source + steps) for source in range(i...  86.5 us
    dynamic_update_slice x2, local copies, waits for them, and re-layouts, place(): lax.dynamic_update_slice(grad_ext, current + own_terms[slot_index], (anch...  28.5 us
    ppermute x6, starting transfers between devices, passed_along(): lax.ppermute(value, axis, [(source, source + steps) for source in range(i...  15.9 us
    dot_general x2, matrix products, transform(): jnp.einsum('ij,mjk->mik', sin_table, stacked, preferred_element_type=jnp....  15.6 us
    dot_general x2, matrix products, transform(): jnp.einsum('ij,mjk->mik', cos_table, stacked, preferred_element_type=jnp....  13.8 us
    gather x6, local copies, waits for them, and re-layouts  11.2 us
    dot_general x2, matrix products, transform(): jnp.einsum('mij,jk->mik', stacked, cos_table, preferred_element_type=jnp....  11.1 us
  transfers between devices with their start and end apart: 11, of which 4 were waited for; matrix products, arithmetic and copies ran while one was open for 12% of the time, Pallas kernels for 0%

commit v1 on v0

v1 whole, which is shorter than its diff:
```python
import functools
import math

import jax
import jax.numpy as jnp
import ml_dtypes
import numpy as np
from jax import lax
from jax.experimental import pallas as pl
from jax.experimental.pallas import tpu as pltpu
from jax.sharding import PartitionSpec as P

CHUNKS = 2
ROWS = 32


def flipped(value, axis, bit):
    mask = 1 << bit
    return lax.ppermute(value, axis, [(at, at ^ mask) for at in range(lax.axis_size(axis))])


def shifted(value, axis, steps):
    count = lax.axis_size(axis)
    first, last = max(0, -steps), min(count, count - steps)
    return lax.ppermute(value, axis, [(at, at + steps) for at in range(first, last)])


def block_tables(length):
    index = np.arange(length)
    angle = (index[:, None] * index[None, :] % length) * (2.0 * math.pi / length)
    scale = 1.0 / math.sqrt(length)
    cos = (np.cos(angle) * scale).astype(np.float32)
    sin = (np.sin(angle) * scale).astype(np.float32)
    ahead = np.block([[cos, sin], [-sin, cos]]).astype(ml_dtypes.bfloat16)
    back = np.block([[cos, -sin], [sin, cos]]).astype(ml_dtypes.bfloat16)
    return ahead, back


def slot_kernel(
    scale, at_ref, piece_ref, probe_ref, amp_ref, ahead_ref, back_ref,
    grad_ref, mode_ref, win, far, stacked, middle,
):
    modes, n = probe_ref.shape[1], probe_ref.shape[2]
    wide = n // 2
    row_at, col_at = at_ref[0], at_ref[1]
    row_back = lax.rem(n - row_at, n)
    col_back = lax.rem(n - col_at, n)
    for part in range(2):
        win[part] = pltpu.roll(pltpu.roll(piece_ref[part], row_back, 0), col_back, 1)

    def products(m, left_ref, right_ref):
        for half in range(2):
            for j in range(2):
                cols = slice(j * wide, (j + 1) * wide)
                middle[:, half * n + j * wide : half * n + (j + 1) * wide] = jnp.dot(
                    left_ref[half * n : (half + 1) * n, :],
                    stacked[:, cols],
                    preferred_element_type=jnp.float32,
                ).astype(jnp.bfloat16)
        for half in range(2):
            for j in range(2):
                far[m, half, :, j * wide : (j + 1) * wide] = jnp.dot(
                    middle[...],
                    right_ref[:, half * n + j * wide : half * n + (j + 1) * wide],
                    preferred_element_type=jnp.float32,
                )

    def rows_of(k):
        return pl.ds(pl.multiple_of(k * ROWS, ROWS), ROWS)

    def lower_of(k):
        return pl.ds(pl.multiple_of(n + k * ROWS, ROWS), ROWS)

    @pl.loop(0, modes)
    def _(m):
        @pl.loop(0, n // ROWS)
        def _(k):
            rows = rows_of(k)
            pr, pi = probe_ref[0, m, rows, :], probe_ref[1, m, rows, :]
            wr, wi = win[0, rows, :], win[1, rows, :]
            stacked[rows, :] = (pr * wr - pi * wi).astype(jnp.bfloat16)
            stacked[lower_of(k), :] = (pr * wi + pi * wr).astype(jnp.bfloat16)

        products(m, ahead_ref, back_ref)

    @pl.loop(0, n // ROWS)
    def _(k):
        rows = rows_of(k)
        total = jnp.zeros((ROWS, n), jnp.float32)
        for m in range(modes):
            total += far[m, 0, rows, :] * far[m, 0, rows, :] + far[m, 1, rows, :] * far[m, 1, rows, :]
        factor = amp_ref[rows, :] * lax.rsqrt(jnp.maximum(total, 1.0)) - 1.0
        for m in range(modes):
            far[m, 0, rows, :] = far[m, 0, rows, :] * factor
            far[m, 1, rows, :] = far[m, 1, rows, :] * factor

    @pl.loop(0, modes)
    def _(m):
        @pl.loop(0, n // ROWS)
        def _(k):
            stacked[rows_of(k), :] = far[m, 0, rows_of(k), :].astype(jnp.bfloat16)
            stacked[lower_of(k), :] = far[m, 1, rows_of(k), :].astype(jnp.bfloat16)

        products(m, back_ref, ahead_ref)

    @pl.loop(0, n // ROWS)
    def _(k):
        rows = rows_of(k)
        wr, wi = win[0, rows, :] * scale, win[1, rows, :] * scale
        grad_re = jnp.zeros((ROWS, n), jnp.float32)
        grad_im = jnp.zeros((ROWS, n), jnp.float32)
        for m in range(modes):
            br, bi = far[m, 0, rows, :], far[m, 1, rows, :]
            pr, pi = probe_ref[0, m, rows, :], probe_ref[1, m, rows, :]
            mode_ref[0, m, rows, :] = wr * br + wi * bi
            mode_ref[1, m, rows, :] = wr * bi - wi * br
            grad_re += pr * br + pi * bi
            grad_im += pr * bi - pi * br
        win[0, rows, :] = grad_re
        win[1, rows, :] = grad_im

    for part in range(2):
        grad_ref[part] = pltpu.roll(pltpu.roll(win[part], row_at, 0), col_at, 1)


def slot_terms(at, piece, probe_modes, measured, scale):
    modes, n = probe_modes.shape[1], probe_modes.shape[2]
    ahead, back = block_tables(n)
    vmem = pl.BlockSpec(memory_space=pltpu.VMEM)
    return pl.pallas_call(
        functools.partial(slot_kernel, scale),
        out_shape=(
            jax.ShapeDtypeStruct((2, n, n), jnp.float32),
            jax.ShapeDtypeStruct((2, modes, n, n), jnp.float32),
        ),
        in_specs=[pl.BlockSpec(memory_space=pltpu.SMEM)] + [vmem] * 5,
        out_specs=(vmem, vmem),
        scratch_shapes=[
            pltpu.VMEM((2, n, n), jnp.float32),
            pltpu.VMEM((modes, 2, n, n), jnp.float32),
            pltpu.VMEM((2 * n, n), jnp.bfloat16),
            pltpu.VMEM((n, 2 * n), jnp.bfloat16),
        ],
        compiler_params=pltpu.CompilerParams(vmem_limit_bytes=50 * 2**20),
        cost_estimate=pl.CostEstimate(
            flops=modes * 32 * n**3, bytes_accessed=24 * 2**20, transcendentals=n * n
        ),
    )(at, piece, probe_modes, measured, jnp.asarray(ahead), jnp.asarray(back))


def summed(value, bits):
    if not bits:
        return value
    axis, bit = bits[0]
    upper = (lax.axis_index(axis) >> bit) & 1 == 1
    half = value.shape[0] // 2
    first, second = value[:half], value[half:]
    got = flipped(jnp.where(upper, first, second), axis, bit)
    kept = jnp.where(upper, second, first) + got
    rest = bits[1:]
    if len(bits) == SPLIT_AT[0]:
        quarter = half // 2
        swapped = [rest[1], rest[0]] + rest[2:]
        done = jnp.concatenate([summed(kept[:quarter], rest), summed(kept[quarter:], swapped)])
    else:
        done = summed(kept, rest)
    other = flipped(done, axis, bit)
    return jnp.concatenate([jnp.where(upper, other, done), jnp.where(upper, done, other)])


SPLIT_AT = [0]


def sum_all(value):
    tx_bits = lax.axis_size("tx").bit_length() - 1
    ty_bits = lax.axis_size("ty").bit_length() - 1
    bits = [("tx", bit) for bit in range(tx_bits)] + [("ty", bit) for bit in reversed(range(ty_bits))]
    SPLIT_AT[0] = len(bits)
    flat = value.reshape(-1, value.shape[-1])
    return summed(flat, bits).reshape(value.shape)


def local(specimen, probe_modes, amplitude, offsets, live_slots):
    width = probe_modes.shape[2]
    slots = live_slots.shape[0]
    n_tx = lax.axis_size("tx")
    devices_all = lax.axis_size("ty") * n_tx
    size = width // CHUNKS
    col = lax.axis_index("tx").astype(jnp.int32)
    mate = col ^ 1
    even_at = range(0, n_tx - 2, 2)

    lower = [
        shifted(specimen[:, k * size : (k + 1) * size, :], "ty", -1) for k in range(CHUNKS)
    ]
    meta = jnp.concatenate([offsets.reshape(-1), jnp.sum(live_slots).reshape(1)])
    mate_meta = flipped(meta, "tx", 0)

    def item(held, held_col, others, others_col):
        own = held[4] >= 1
        return jnp.stack([
            jnp.where(own, held[0], others[2]),
            jnp.where(own, held[1], others[3]),
            jnp.where(own, held_col, others_col),
        ])

    mine = item(meta, col, mate_meta, mate)
    theirs = item(mate_meta, mate, meta, col)
    before = lax.ppermute(jnp.stack([mine, theirs]), "tx", [(at, at + 2) for at in even_at])
    measured = jnp.where(meta[4] >= 1, amplitude[0], flipped(amplitude[1], "tx", 0))

    p_at = lax.broadcasted_iota(jnp.int32, (1, 1, width), 2)

    def q_at(k):
        return lax.broadcasted_iota(jnp.int32, (1, size, 1), 1) + k * size

    def picked(k, work):
        q = q_at(k)
        upper_rows = specimen[:, k * size : (k + 1) * size, :]
        lower_rows = specimen[:, width + k * size : width + (k + 1) * size, :]
        own_rows = jnp.where(q >= work[0], upper_rows, lower_rows)
        return jnp.where(q + width < work[0], lower[k], own_rows)

    pieces = []
    for k in range(CHUNKS):
        next_even = lax.ppermute(picked(k, before[0]), "tx", [(at + 2, at) for at in even_at])
        next_odd = lax.ppermute(picked(k, before[1]), "tx", [(at + 2, at + 1) for at in even_at])
        from_next = next_even + next_odd
        from_mate = flipped(picked(k, theirs), "tx", 0)
        own = picked(k, mine)

        def strip(tile):
            return jnp.where(tile == col, own, jnp.where(tile == mate, from_mate, from_next))

        pieces.append(jnp.where(p_at >= mine[1], strip(mine[2]), strip(mine[2] + 1)))
    piece = jnp.concatenate(pieces, axis=1)

    at = jnp.stack([lax.rem(mine[0], width), lax.rem(mine[1], width)])
    scale = 1.0 / math.sqrt(slots * devices_all)
    grad, mode_terms = slot_terms(at, piece, probe_modes, measured, scale)

    def col_mask(work):
        return ((work[2] == col) & (p_at >= work[1])) | ((work[2] + 1 == col) & (p_at < work[1]))

    works = [mine, theirs, before[0], before[1]]
    masks = [col_mask(work) for work in works]
    tops, bottoms, aboves = [], [], []
    for k in range(CHUNKS):
        q = q_at(k)
        mine_k = grad[:, k * size : (k + 1) * size, :]
        terms = [
            mine_k,
            flipped(mine_k, "tx", 0),
            lax.ppermute(mine_k, "tx", [(at, at + 2) for at in even_at]),
            lax.ppermute(mine_k, "tx", [(at + 1, at + 2) for at in even_at]),
        ]
        top = bottom = beyond = jnp.zeros((), jnp.float32)
        for term, work, mask in zip(terms, works, masks):
            row = work[0]
            top += jnp.where(mask & (q >= row), term, 0.0)
            bottom += jnp.where(mask & (q < row) & (q + width >= row), term, 0.0)
            beyond += jnp.where(mask & (q + width < row), term, 0.0)
        aboves.append(shifted(beyond, "ty", 1))
        tops.append(top)
        bottoms.append(bottom)
    probe_grad = sum_all(mode_terms)
    tops = [top + above for top, above in zip(tops, aboves)]
    return (jnp.concatenate(tops + bottoms, axis=1), probe_grad)


def solution(mesh):
    return jax.shard_map(
        local,
        mesh=mesh,
        in_specs=(
            P(None, "ty", "tx"),
            P(),
            P(("ty", "tx"), None, None),
            P(("ty", "tx"), None),
            P(("ty", "tx")),
        ),
        out_specs=(P(None, "ty", "tx"), P()),
        check_vma=False,
    )
```

time: 541 us -> 360 us (0.67); the launches traced: 533 us -> 359 us
  waiting for transfers between devices: 298 us -> 200 us
  local copies, waits for them, and re-layouts: 73.9 us -> 5.25 us
  matrix products: 51.1 us -> 0 us
  starting transfers between devices: 17.4 us -> 59.8 us
  Pallas kernels: 0 us -> 27.2 us
  other arithmetic: 67.9 us -> 56.5 us
  loops' own time: 8.19 us -> 0 us
  between operations: 16.5 us -> 10.6 us
    psum x1 -> x0, waiting for transfers between devices: 208 us -> none  [local(): probe_total = lax.psum(jnp.sum(probe_terms, axis=0), ('ty', 'tx'))]
    ppermute x10 -> x37, waiting for transfers between devices: 89.4 us -> 200 us  [the longest x24 68.6 us: flipped(): lax.ppermute(value, axis, [(at, at ^ mask) for at in range(lax.axis_size(...]
    dot_general x8 -> x0, matrix products: 51.1 us -> none  [the longest x2 15.6 us: transform(): jnp.einsum('ij,mjk->mik', sin_table, stacked, preferred_element_type=jnp....]
    ppermute x10 -> x37, starting transfers between devices: 17.4 us -> 59.8 us  [the longest x24 31 us: flipped(): lax.ppermute(value, axis, [(at, at ^ mask) for at in range(lax.axis_size(...]
    dynamic_update_slice x2 -> x0, local copies, waits for them, and re-layouts: 28.5 us -> none  [place(): lax.dynamic_update_slice(grad_ext, current + own_terms[slot_index], (anch...]
    pallas_call x0 -> x1, Pallas kernels: none -> 27.2 us  [slot_terms(): pl.pallas_call(functools.partial(slot_kernel, scale), out_shape=(jax.Shap...]
    select_n x4 -> x22, other arithmetic: 4.08 us -> 23.3 us  [the longest x1 6.89 us: summed(): kept = jnp.where(upper, second, first) + got]
    convert_element_type x5 -> x0, other arithmetic: 15.7 us -> none  [the longest x2 8.7 us: transform(): (cos_part[:, :, :length] + orient * sin_part[:, :, length:]).astype(jnp.b...]
  transfers between devices with their start and end apart: 11 -> 37, of which waited for: 4 -> 18; matrix products, arithmetic and copies ran while one was open for 12% -> 9% of each run, Pallas kernels for 0% -> 0%
where the time goes in v1:
time: 360 us; the launch traced here: 359 us
  waiting for transfers between devices  200 us (56%)
  starting transfers between devices  59.8 us (17%)
  other arithmetic  56.5 us (16%)
  Pallas kernels  27.2 us (8%)
  between operations  10.6 us (3%)
  local copies, waits for them, and re-layouts  5.25 us (1%)
    ppermute x24, waiting for transfers between devices, flipped(): lax.ppermute(value, axis, [(at, at ^ mask) for at in range(lax.axis_size(...  68.6 us
    ppermute x4, waiting for transfers between devices, shifted(): lax.ppermute(value, axis, [(at, at + steps) for at in range(first, last)])  61.3 us
    ppermute x2, waiting for transfers between devices, local(): lax.ppermute(picked(k, before[1]), 'tx', [(at + 2, at + 1) for at in even...  49.2 us
    ppermute x24, starting transfers between devices, flipped(): lax.ppermute(value, axis, [(at, at ^ mask) for at in range(lax.axis_size(...  31 us
    pallas_call x1, Pallas kernels, slot_terms(): pl.pallas_call(functools.partial(slot_kernel, scale), out_shape=(jax.Shap...  27.2 us
    ppermute x2, waiting for transfers between devices, local(): lax.ppermute(mine_k, 'tx', [(at + 1, at + 2) for at in even_at])  20.7 us
    ppermute x2, starting transfers between devices, local(): lax.ppermute(mine_k, 'tx', [(at + 1, at + 2) for at in even_at])  11.6 us
    ppermute x4, starting transfers between devices, shifted(): lax.ppermute(value, axis, [(at, at + steps) for at in range(first, last)])  9.03 us
  transfers between devices with their start and end apart: 37, of which 18 were waited for; matrix products, arithmetic and copies ran while one was open for 9% of the time, Pallas kernels for 0%

profile of v1, /device:TPU:27, one launch (start us, length us, event | category | flops | bytes accessed | tf_op | source)
XLA Modules:
  0.0 359.1 jit_solution(2048449857882603136)
XLA Ops:
  5.4 2.1 collective-permute-start.1
  19.5 10.6 %collective-permute-done.1 = f32[2,256,512]{2,1,0:T(8,128)S(1)} collective-permute-done((f32[2,256,512]{2,1,0:T(8,128)S(1)}, f32[2,256,512]{2,1,0:T(8,128)S(1)}, u32[]{:S(2)}, u32[]{:S(2)}) %collective-permute-start.1) | collective-permute-done | bytes 1048608 | tf_op jit(solution)/shard_map/ppermute | solution.py:25
  30.0 2.9 select_select_fusion.5
  36.7 25.2 %collective-permute-done.5 = f32[2,256,512]{2,1,0:T(8,128)} collective-permute-done((f32[2,256,512]{2,1,0:T(8,128)S(1)}, f32[2,256,512]{2,1,0:T(8,128)}, u32[]{:S(2)}, u32[]{:S(2)}) %collective-permute-start.5) | collective-permute-done | bytes 1048608 | tf_op jit(solution)/shard_map/ppermute | solution.py:227
  61.9 3.4 select_select_fusion.4
  65.4 4.3 %collective-permute-start.6 = (f32[2,256,512]{2,1,0:T(8,128)S(1)}, f32[2,256,512]{2,1,0:T(8,128)S(1)}, u32[]{:S(2)}, u32[]{:S(2)}) collective-permute-start(f32[2,256,512]{2,1,0:T(8,128)S(1)} %get-tuple-element.21), channel_id=1, source_target_pairs={{8,0},{16,8},{24,16},{9,1},{17,9},{25,17},{10,2},{18,10},{26,18},{... | collective-permute-start | bytes 3145736 | tf_op jit(solution)/shard_map/ppermute | solution.py:25
  73.4 17.4 %collective-permute-done.6 = f32[2,256,512]{2,1,0:T(8,128)S(1)} collective-permute-done((f32[2,256,512]{2,1,0:T(8,128)S(1)}, f32[2,256,512]{2,1,0:T(8,128)S(1)}, u32[]{:S(2)}, u32[]{:S(2)}) %collective-permute-start.6) | collective-permute-done | bytes 1048608 | tf_op jit(solution)/shard_map/ppermute | solution.py:25
  97.6 23.9 %collective-permute-done.9 = f32[2,256,512]{2,1,0:T(8,128)} collective-permute-done((f32[2,256,512]{2,1,0:T(8,128)S(1)}, f32[2,256,512]{2,1,0:T(8,128)}, u32[]{:S(2)}, u32[]{:S(2)}) %collective-permute-start.9) | collective-permute-done | bytes 1048608 | tf_op jit(solution)/shard_map/ppermute | solution.py:227
  121.5 2.9 select_select_fusion
  126.0 27.2 %shard_map.86 = (f32[2,512,512]{2,1,0:T(8,128)S(1)}, f32[2,3,512,512]{3,2,1,0:T(8,128)}) custom-call(s32[2]{0:T(128)S(1)} %pad_add_fusion.2.at_ref, f32[2,512,512]{2,1,0:T(8,128)} %pad_maximum_fusion.3.piece_ref, f32[2,3,512,512]{3,2,1,0:T(8,128)} %probe_ref.1, f32[512,512]{1,0:T(8,128)S(1)} %bitcast_select_fusion.amp_ref, ...), custom_call_target="tpu_custom_call" | custom-call | flops 12884901888 | bytes 25165824 | tf_op jit(solution)/shard_map/pallas_call | solution.py:130
  153.1 6.9 %slice_select_fusion.1 = (f32[1,3,512,512]{3,2,1,0:T(8,128)}, f32[1,3,512,512]{3,2,1,0:T(8,128)}) fusion(f32[2,3,512,512]{3,2,1,0:T(8,128)} %get-tuple-element.5, pred[]{:T(512)S(6)} %eq.65), kind=kLoop, calls=%fused_computation.5 | loop fusion | flops 1572864 | bytes 12582913 | tf_op jit(solution)/shard_map/jit(_where)/select_n | solution.py:159
  168.6 3.6 %bitcast_add_fusion = f32[1536,512]{1,0:T(8,128)S(1)} fusion(f32[1536,512]{1,0:T(8,128)} %collective-permute-done.19, f32[1,3,512,512]{3,2,1,0:T(8,128)} %get-tuple-element.8), kind=kLoop, calls=%fused_computation.3 | loop fusion | flops 786432 | bytes 9437184 | tf_op jit(solution)/shard_map/add | solution.py:159
  178.1 13.2 %collective-permute-done.20 = f32[384,512]{1,0:T(8,128)S(1)} collective-permute-done((f32[384,512]{1,0:T(8,128)S(1)}, f32[384,512]{1,0:T(8,128)S(1)}, u32[]{:S(2)}, u32[]{:S(2)}) %collective-permute-start.20) | collective-permute-done | bytes 786464 | tf_op jit(solution)/shard_map/ppermute | solution.py:19
  193.8 2.0 collective-permute-start.11
  196.5 4.8 %collective-permute-start.13 = (f32[2,256,512]{2,1,0:T(8,128)S(1)}, f32[2,256,512]{2,1,0:T(8,128)S(1)}, u32[]{:S(2)}, u32[]{:S(2)}) collective-permute-start(f32[2,256,512]{2,1,0:T(8,128)S(1)} %slice.194), channel_id=1, source_target_pairs={{1,2},{3,4},{5,6},{9,10},{11,12},{13,14},{17,18},{19,20},{21,22},{... | collective-permute-start | bytes 3145736 | tf_op jit(solution)/shard_map/ppermute | solution.py:255
  204.9 26.6 %collective-permute-done.29 = f32[192,512]{1,0:T(8,128)S(1)} collective-permute-done((f32[192,512]{1,0:T(8,128)S(1)}, f32[192,512]{1,0:T(8,128)S(1)}, u32[]{:S(2)}, u32[]{:S(2)}) %collective-permute-start.29) | collective-permute-done | bytes 393248 | tf_op jit(solution)/shard_map/ppermute | solution.py:19
  231.6 2.1 collective-permute-start.30
  234.1 7.8 %collective-permute-done.30 = f32[96,512]{1,0:T(8,128)S(1)} collective-permute-done((f32[96,512]{1,0:T(8,128)S(1)}, f32[96,512]{1,0:T(8,128)S(1)}, u32[]{:S(2)}, u32[]{:S(2)}) %collective-permute-start.30) | collective-permute-done | bytes 196640 | tf_op jit(solution)/shard_map/ppermute | solution.py:19
  243.6 3.2 collective-permute-done.31
  247.6 2.3 collective-permute-start.25
  251.9 11.5 %collective-permute-done.25 = f32[96,512]{1,0:T(8,128)S(1)} collective-permute-done((f32[96,512]{1,0:T(8,128)S(1)}, f32[96,512]{1,0:T(8,128)S(1)}, u32[]{:S(2)}, u32[]{:S(2)}) %collective-permute-start.25) | collective-permute-done | bytes 196640 | tf_op jit(solution)/shard_map/ppermute | solution.py:19
  267.7 3.6 %collective-permute-start.34 = (f32[192,512]{1,0:T(8,128)S(1)}, f32[192,512]{1,0:T(8,128)S(1)}, u32[]{:S(2)}, u32[]{:S(2)}) collective-permute-start(f32[192,512]{1,0:T(8,128)S(1)} %pad_maximum_fusion.7), channel_id=1, source_target_pairs={{0,2},{1,3},{2,0},{3,1},{4,6},{5,7},{6,4},{7,5},{8,10},{9,11},{10,... | collective-permute-start | bytes 1179656 | tf_op jit(solution)/shard_map/ppermute | solution.py:19
  272.5 4.9 %collective-permute-start.27 = (f32[384,512]{1,0:T(8,128)S(1)}, f32[384,512]{1,0:T(8,128)S(1)}, u32[]{:S(2)}, u32[]{:S(2)}) collective-permute-start(f32[384,512]{1,0:T(8,128)S(1)} %pad_maximum_fusion.4), channel_id=1, source_target_pairs={{0,2},{1,3},{2,0},{3,1},{4,6},{5,7},{6,4},{7,5},{8,10},{9,11},{10,... | collective-permute-start | bytes 2359304 | tf_op jit(solution)/shard_map/ppermute | solution.py:19
  277.4 2.9 collective-permute-done.34
  280.5 8.3 %collective-permute-done.14 = f32[2,256,512]{2,1,0:T(8,128)S(1)} collective-permute-done((f32[2,256,512]{2,1,0:T(8,128)S(1)}, f32[2,256,512]{2,1,0:T(8,128)S(1)}, u32[]{:S(2)}, u32[]{:S(2)}) %collective-permute-start.14) | collective-permute-done | bytes 1048608 | tf_op jit(solution)/shard_map/ppermute | solution.py:25
  289.7 3.9 %collective-permute-start.15 = (f32[2,256,512]{2,1,0:T(8,128)S(1)}, f32[2,256,512]{2,1,0:T(8,128)S(1)}, u32[]{:S(2)}, u32[]{:S(2)}) collective-permute-start(f32[2,256,512]{2,1,0:T(8,128)S(1)} %get-tuple-element.26), channel_id=1, source_target_pairs={{0,1},{1,0},{2,3},{3,2},{4,5},{5,4},{6,7},{7,6},{8,9},{9,8},{10,11... | collective-permute-start | bytes 3145736 | tf_op jit(solution)/shard_map/ppermute | solution.py:19
  294.4 6.9 %collective-permute-start.17 = (f32[2,256,512]{2,1,0:T(8,128)S(1)}, f32[2,256,512]{2,1,0:T(8,128)S(1)}, u32[]{:S(2)}, u32[]{:S(2)}) collective-permute-start(f32[2,256,512]{2,1,0:T(8,128)S(1)} %get-tuple-element.26), channel_id=1, source_target_pairs={{1,2},{3,4},{5,6},{9,10},{11,12},{13,14},{17,18},{19,20},{21,22},{... | collective-permute-start | bytes 3145736 | tf_op jit(solution)/shard_map/ppermute | solution.py:255
  302.1 20.7 %collective-permute-done.17 = f32[2,256,512]{2,1,0:T(8,128)S(1)} collective-permute-done((f32[2,256,512]{2,1,0:T(8,128)S(1)}, f32[2,256,512]{2,1,0:T(8,128)S(1)}, u32[]{:S(2)}, u32[]{:S(2)}) %collective-permute-start.17) | collective-permute-done | bytes 1048608 | tf_op jit(solution)/shard_map/ppermute | solution.py:255
  324.7 25.0 %collective-permute-done.18 = f32[2,256,512]{2,1,0:T(8,128)S(1)} collective-permute-done((f32[2,256,512]{2,1,0:T(8,128)S(1)}, f32[2,256,512]{2,1,0:T(8,128)S(1)}, u32[]{:S(2)}, u32[]{:S(2)}) %collective-permute-start.18) | collective-permute-done | bytes 1048608 | tf_op jit(solution)/shard_map/ppermute | solution.py:25
  350.6 2.5 pad_maximum_fusion.1
  353.0 2.7 broadcast_select_fusion.1
  355.7 3.4 pad_maximum_fusion
  (162 shorter events, 59.8 us)
Async XLA Ops:
  3.4 5.4 %collective-permute-start = (s32[5]{0:T(128)S(1)}, s32[5]{0:T(128)S(1)}, u32[]{:S(2)}, u32[]{:S(2)}) collective-permute-start(s32[5]{0:T(128)S(1)} %pad_add_fusion.1), channel_id=1, source_target_pairs={{0,1},{1,0},{2,3},{3,2},{4,5},{5,4},{6,7},{7,6},{8,9},{9,8},{10,11... | collective-permute-start | bytes 68 | tf_op jit(solution)/shard_map/ppermute | solution.py:19
  5.4 24.6 %collective-permute-start.1 = (f32[2,256,512]{2,1,0:T(8,128)S(1)}, f32[2,256,512]{2,1,0:T(8,128)S(1)}, u32[]{:S(2)}, u32[]{:S(2)}) collective-permute-start(f32[2,256,512]{2,1,0:T(8,128)S(1)} %slice.181), channel_id=1, source_target_pairs={{8,0},{16,8},{24,16},{9,1},{17,9},{25,17},{10,2},{18,10},{26,18},{... | collective-permute-start | bytes 3145736 | tf_op jit(solution)/shard_map/ppermute | solution.py:25
  35.3 26.6 %collective-permute-start.5 = (f32[2,256,512]{2,1,0:T(8,128)S(1)}, f32[2,256,512]{2,1,0:T(8,128)}, u32[]{:S(2)}, u32[]{:S(2)}) collective-permute-start(f32[2,256,512]{2,1,0:T(8,128)S(1)} %get-tuple-element.14), channel_id=1, source_target_pairs={{2,1},{4,3},{6,5},{10,9},{12,11},{14,13},{18,17},{20,19},{22,21},{... | collective-permute-start | bytes 3145736 | tf_op jit(solution)/shard_map/ppermute | solution.py:227
  65.4 25.4 %collective-permute-start.6 = (f32[2,256,512]{2,1,0:T(8,128)S(1)}, f32[2,256,512]{2,1,0:T(8,128)S(1)}, u32[]{:S(2)}, u32[]{:S(2)}) collective-permute-start(f32[2,256,512]{2,1,0:T(8,128)S(1)} %get-tuple-element.21), channel_id=1, source_target_pairs={{8,0},{16,8},{24,16},{9,1},{17,9},{25,17},{10,2},{18,10},{26,18},{... | collective-permute-start | bytes 3145736 | tf_op jit(solution)/shard_map/ppermute | solution.py:25
  70.7 25.0 %collective-permute-start.10 = (f32[512,512]{1,0:T(8,128)}, f32[512,512]{1,0:T(8,128)}, u32[]{:S(2)}, u32[]{:S(2)}) collective-permute-start(f32[512,512]{1,0:T(8,128)} %slice_bitcast_fusion), channel_id=1, source_target_pairs={{0,1},{1,0},{2,3},{3,2},{4,5},{5,4},{6,7},{7,6},{8,9},{9,8},{10,11... | collective-permute-start | bytes 3145736 | tf_op jit(solution)/shard_map/ppermute | solution.py:19
  92.5 5.1 %collective-permute-start.7 = (f32[2,256,512]{2,1,0:T(8,128)}, f32[2,256,512]{2,1,0:T(8,128)}, u32[]{:S(2)}, u32[]{:S(2)}) collective-permute-start(f32[2,256,512]{2,1,0:T(8,128)} %get-tuple-element.19), channel_id=1, source_target_pairs={{0,1},{1,0},{2,3},{3,2},{4,5},{5,4},{6,7},{7,6},{8,9},{9,8},{10,11... | collective-permute-start | bytes 3145736 | tf_op jit(solution)/shard_map/ppermute | solution.py:19
  92.6 5.0 %collective-permute-start.8 = (f32[2,256,512]{2,1,0:T(8,128)}, f32[2,256,512]{2,1,0:T(8,128)}, u32[]{:S(2)}, u32[]{:S(2)}) collective-permute-start(f32[2,256,512]{2,1,0:T(8,128)} %get-tuple-element.18), channel_id=1, source_target_pairs={{2,0},{4,2},{6,4},{10,8},{12,10},{14,12},{18,16},{20,18},{22,20},{... | collective-permute-start | bytes 3145736 | tf_op jit(solution)/shard_map/ppermute | solution.py:226
  94.2 27.3 %collective-permute-start.9 = (f32[2,256,512]{2,1,0:T(8,128)S(1)}, f32[2,256,512]{2,1,0:T(8,128)}, u32[]{:S(2)}, u32[]{:S(2)}) collective-permute-start(f32[2,256,512]{2,1,0:T(8,128)S(1)} %get-tuple-element.17), channel_id=1, source_target_pairs={{2,1},{4,3},{6,5},{10,9},{12,11},{14,13},{18,17},{20,19},{22,21},{... | collective-permute-start | bytes 3145736 | tf_op jit(solution)/shard_map/ppermute | solution.py:227
  160.0 8.6 %collective-permute-start.19 = (f32[1536,512]{1,0:T(8,128)}, f32[1536,512]{1,0:T(8,128)}, u32[]{:S(2)}, u32[]{:S(2)}) collective-permute-start(f32[1536,512]{1,0:T(8,128)} %bitcast.29), channel_id=1, source_target_pairs={{0,1},{1,0},{2,3},{3,2},{4,5},{5,4},{6,7},{7,6},{8,9},{9,8},{10,11... | collective-permute-start | bytes 9437192 | tf_op jit(solution)/shard_map/ppermute | solution.py:19
  172.6 18.7 %collective-permute-start.20 = (f32[384,512]{1,0:T(8,128)S(1)}, f32[384,512]{1,0:T(8,128)S(1)}, u32[]{:S(2)}, u32[]{:S(2)}) collective-permute-start(f32[384,512]{1,0:T(8,128)S(1)} %get-tuple-element.24), channel_id=1, source_target_pairs={{0,2},{1,3},{2,0},{3,1},{4,6},{5,7},{6,4},{7,5},{8,10},{9,11},{10,... | collective-permute-start | bytes 2359304 | tf_op jit(solution)/shard_map/ppermute | solution.py:19
  172.7 18.7 %collective-permute-start.28 = (f32[384,512]{1,0:T(8,128)S(1)}, f32[384,512]{1,0:T(8,128)S(1)}, u32[]{:S(2)}, u32[]{:S(2)}) collective-permute-start(f32[384,512]{1,0:T(8,128)S(1)} %get-tuple-element.25), channel_id=1, source_target_pairs={{0,4},{1,5},{2,6},{3,7},{4,0},{5,1},{6,2},{7,3},{8,12},{9,13},{10,... | collective-permute-start | bytes 2359304 | tf_op jit(solution)/shard_map/ppermute | solution.py:19
  192.0 10.9 %collective-permute-start.21 = (f32[192,512]{1,0:T(8,128)S(1)}, f32[192,512]{1,0:T(8,128)S(1)}, u32[]{:S(2)}, u32[]{:S(2)}) collective-permute-start(f32[192,512]{1,0:T(8,128)S(1)} %slice_select_fusion.5), channel_id=1, source_target_pairs={{0,4},{1,5},{2,6},{3,7},{4,0},{5,1},{6,2},{7,3},{8,12},{9,13},{10,... | collective-permute-start | bytes 1179656 | tf_op jit(solution)/shard_map/ppermute | solution.py:19
  193.8 70.7 %collective-permute-start.11 = (f32[2,256,512]{2,1,0:T(8,128)S(1)}, f32[2,256,512]{2,1,0:T(8,128)S(1)}, u32[]{:S(2)}, u32[]{:S(2)}) collective-permute-start(f32[2,256,512]{2,1,0:T(8,128)S(1)} %slice.194), channel_id=1, source_target_pairs={{0,1},{1,0},{2,3},{3,2},{4,5},{5,4},{6,7},{7,6},{8,9},{9,8},{10,11... | collective-permute-start | bytes 3145736 | tf_op jit(solution)/shard_map/ppermute | solution.py:19
  195.8 68.7 %collective-permute-start.12 = (f32[2,256,512]{2,1,0:T(8,128)S(1)}, f32[2,256,512]{2,1,0:T(8,128)S(1)}, u32[]{:S(2)}, u32[]{:S(2)}) collective-permute-start(f32[2,256,512]{2,1,0:T(8,128)S(1)} %slice.194), channel_id=1, source_target_pairs={{0,2},{2,4},{4,6},{8,10},{10,12},{12,14},{16,18},{18,20},{20,22},{... | collective-permute-start | bytes 3145736 | tf_op jit(solution)/shard_map/ppermute | solution.py:254
  196.5 68.0 %collective-permute-start.13 = (f32[2,256,512]{2,1,0:T(8,128)S(1)}, f32[2,256,512]{2,1,0:T(8,128)S(1)}, u32[]{:S(2)}, u32[]{:S(2)}) collective-permute-start(f32[2,256,512]{2,1,0:T(8,128)S(1)} %slice.194), channel_id=1, source_target_pairs={{1,2},{3,4},{5,6},{9,10},{11,12},{13,14},{17,18},{19,20},{21,22},{... | collective-permute-start | bytes 3145736 | tf_op jit(solution)/shard_map/ppermute | solution.py:255
  201.4 30.1 %collective-permute-start.29 = (f32[192,512]{1,0:T(8,128)S(1)}, f32[192,512]{1,0:T(8,128)S(1)}, u32[]{:S(2)}, u32[]{:S(2)}) collective-permute-start(f32[192,512]{1,0:T(8,128)S(1)} %slice_select_fusion.4), channel_id=1, source_target_pairs={{0,2},{1,3},{2,0},{3,1},{4,6},{5,7},{6,4},{7,5},{8,10},{9,11},{10,... | collective-permute-start | bytes 1179656 | tf_op jit(solution)/shard_map/ppermute | solution.py:19
  203.0 30.8 %collective-permute-start.22 = (f32[96,512]{1,0:T(8,128)S(1)}, f32[96,512]{1,0:T(8,128)S(1)}, u32[]{:S(2)}, u32[]{:S(2)}) collective-permute-start(f32[96,512]{1,0:T(8,128)S(1)} %slice_select_fusion.7), channel_id=1, source_target_pairs={{0,16},{8,24},{16,0},{24,8},{1,17},{9,25},{17,1},{25,9},{2,18},{10... | collective-permute-start | bytes 589832 | tf_op jit(solution)/shard_map/ppermute | solution.py:19
  231.6 10.2 %collective-permute-start.30 = (f32[96,512]{1,0:T(8,128)S(1)}, f32[96,512]{1,0:T(8,128)S(1)}, u32[]{:S(2)}, u32[]{:S(2)}) collective-permute-start(f32[96,512]{1,0:T(8,128)S(1)} %slice_select_fusion.6), channel_id=1, source_target_pairs={{0,16},{8,24},{16,0},{24,8},{1,17},{9,25},{17,1},{25,9},{2,18},{10... | collective-permute-start | bytes 589832 | tf_op jit(solution)/shard_map/ppermute | solution.py:19
  233.9 8.2 %collective-permute-start.23 = (f32[48,512]{1,0:T(8,128)S(1)}, f32[48,512]{1,0:T(8,128)S(1)}, u32[]{:S(2)}, u32[]{:S(2)}) collective-permute-start(f32[48,512]{1,0:T(8,128)S(1)} %slice_select_fusion.9), channel_id=1, source_target_pairs={{0,8},{8,0},{16,24},{24,16},{1,9},{9,1},{17,25},{25,17},{2,10},{10... | collective-permute-start | bytes 294920 | tf_op jit(solution)/shard_map/ppermute | solution.py:19
  242.1 5.5 %collective-permute-start.24 = (f32[48,512]{1,0:T(8,128)S(1)}, f32[48,512]{1,0:T(8,128)S(1)}, u32[]{:S(2)}, u32[]{:S(2)}) collective-permute-start(f32[48,512]{1,0:T(8,128)S(1)} %select_add_fusion.11), channel_id=1, source_target_pairs={{0,8},{8,0},{16,24},{24,16},{1,9},{9,1},{17,25},{25,17},{2,10},{10... | collective-permute-start | bytes 294920 | tf_op jit(solution)/shard_map/ppermute | solution.py:19
  247.6 15.8 %collective-permute-start.25 = (f32[96,512]{1,0:T(8,128)S(1)}, f32[96,512]{1,0:T(8,128)S(1)}, u32[]{:S(2)}, u32[]{:S(2)}) collective-permute-start(f32[96,512]{1,0:T(8,128)S(1)} %pad_maximum_fusion.8), channel_id=1, source_target_pairs={{0,16},{8,24},{16,0},{24,8},{1,17},{9,25},{17,1},{25,9},{2,18},{10... | collective-permute-start | bytes 589832 | tf_op jit(solution)/shard_map/ppermute | solution.py:19
  250.4 17.2 %collective-permute-start.33 = (f32[96,512]{1,0:T(8,128)S(1)}, f32[96,512]{1,0:T(8,128)S(1)}, u32[]{:S(2)}, u32[]{:S(2)}) collective-permute-start(f32[96,512]{1,0:T(8,128)S(1)} %pad_maximum_fusion.9), channel_id=1, source_target_pairs={{0,16},{8,24},{16,0},{24,8},{1,17},{9,25},{17,1},{25,9},{2,18},{10... | collective-permute-start | bytes 589832 | tf_op jit(solution)/shard_map/ppermute | solution.py:19
  263.5 8.8 %collective-permute-start.26 = (f32[192,512]{1,0:T(8,128)S(1)}, f32[192,512]{1,0:T(8,128)S(1)}, u32[]{:S(2)}, u32[]{:S(2)}) collective-permute-start(f32[192,512]{1,0:T(8,128)S(1)} %pad_maximum_fusion.6), channel_id=1, source_target_pairs={{0,4},{1,5},{2,6},{3,7},{4,0},{5,1},{6,2},{7,3},{8,12},{9,13},{10,... | collective-permute-start | bytes 1179656 | tf_op jit(solution)/shard_map/ppermute | solution.py:19
  265.2 23.6 %collective-permute-start.14 = (f32[2,256,512]{2,1,0:T(8,128)S(1)}, f32[2,256,512]{2,1,0:T(8,128)S(1)}, u32[]{:S(2)}, u32[]{:S(2)}) collective-permute-start(f32[2,256,512]{2,1,0:T(8,128)S(1)} %select_add_fusion.3), channel_id=1, source_target_pairs={{0,8},{8,16},{16,24},{1,9},{9,17},{17,25},{2,10},{10,18},{18,26},{... | collective-permute-start | bytes 3145736 | tf_op jit(solution)/shard_map/ppermute | solution.py:25
  267.7 12.6 %collective-permute-start.34 = (f32[192,512]{1,0:T(8,128)S(1)}, f32[192,512]{1,0:T(8,128)S(1)}, u32[]{:S(2)}, u32[]{:S(2)}) collective-permute-start(f32[192,512]{1,0:T(8,128)S(1)} %pad_maximum_fusion.7), channel_id=1, source_target_pairs={{0,2},{1,3},{2,0},{3,1},{4,6},{5,7},{6,4},{7,5},{8,10},{9,11},{10,... | collective-permute-start | bytes 1179656 | tf_op jit(solution)/shard_map/ppermute | solution.py:19
  272.5 28.7 %collective-permute-start.27 = (f32[384,512]{1,0:T(8,128)S(1)}, f32[384,512]{1,0:T(8,128)S(1)}, u32[]{:S(2)}, u32[]{:S(2)}) collective-permute-start(f32[384,512]{1,0:T(8,128)S(1)} %pad_maximum_fusion.4), channel_id=1, source_target_pairs={{0,2},{1,3},{2,0},{3,1},{4,6},{5,7},{6,4},{7,5},{8,10},{9,11},{10,... | collective-permute-start | bytes 2359304 | tf_op jit(solution)/shard_map/ppermute | solution.py:19
  280.4 21.0 %collective-permute-start.35 = (f32[384,512]{1,0:T(8,128)S(1)}, f32[384,512]{1,0:T(8,128)S(1)}, u32[]{:S(2)}, u32[]{:S(2)}) collective-permute-start(f32[384,512]{1,0:T(8,128)S(1)} %pad_maximum_fusion.5), channel_id=1, source_target_pairs={{0,4},{1,5},{2,6},{3,7},{4,0},{5,1},{6,2},{7,3},{8,12},{9,13},{10,... | collective-permute-start | bytes 2359304 | tf_op jit(solution)/shard_map/ppermute | solution.py:19
  289.7 12.3 %collective-permute-start.15 = (f32[2,256,512]{2,1,0:T(8,128)S(1)}, f32[2,256,512]{2,1,0:T(8,128)S(1)}, u32[]{:S(2)}, u32[]{:S(2)}) collective-permute-start(f32[2,256,512]{2,1,0:T(8,128)S(1)} %get-tuple-element.26), channel_id=1, source_target_pairs={{0,1},{1,0},{2,3},{3,2},{4,5},{5,4},{6,7},{7,6},{8,9},{9,8},{10,11... | collective-permute-start | bytes 3145736 | tf_op jit(solution)/shard_map/ppermute | solution.py:19
  293.6 8.4 %collective-permute-start.16 = (f32[2,256,512]{2,1,0:T(8,128)S(1)}, f32[2,256,512]{2,1,0:T(8,128)S(1)}, u32[]{:S(2)}, u32[]{:S(2)}) collective-permute-start(f32[2,256,512]{2,1,0:T(8,128)S(1)} %get-tuple-element.26), channel_id=1, source_target_pairs={{0,2},{2,4},{4,6},{8,10},{10,12},{12,14},{16,18},{18,20},{20,22},{... | collective-permute-start | bytes 3145736 | tf_op jit(solution)/shard_map/ppermute | solution.py:254
  294.4 28.4 %collective-permute-start.17 = (f32[2,256,512]{2,1,0:T(8,128)S(1)}, f32[2,256,512]{2,1,0:T(8,128)S(1)}, u32[]{:S(2)}, u32[]{:S(2)}) collective-permute-start(f32[2,256,512]{2,1,0:T(8,128)S(1)} %get-tuple-element.26), channel_id=1, source_target_pairs={{1,2},{3,4},{5,6},{9,10},{11,12},{13,14},{17,18},{19,20},{21,22},{... | collective-permute-start | bytes 3145736 | tf_op jit(solution)/shard_map/ppermute | solution.py:255
  302.0 51.0 %collective-permute-start.36 = (f32[1536,512]{1,0:T(8,128)S(1)}, f32[1536,512]{1,0:T(8,128)}, u32[]{:S(2)}, u32[]{:S(2)}) collective-permute-start(f32[1536,512]{1,0:T(8,128)S(1)} %pad_maximum_fusion.2), channel_id=1, source_target_pairs={{0,1},{1,0},{2,3},{3,2},{4,5},{5,4},{6,7},{7,6},{8,9},{9,8},{10,11... | collective-permute-start | bytes 9437192 | tf_op jit(solution)/shard_map/ppermute | solution.py:19
  323.4 26.3 %collective-permute-start.18 = (f32[2,256,512]{2,1,0:T(8,128)S(1)}, f32[2,256,512]{2,1,0:T(8,128)S(1)}, u32[]{:S(2)}, u32[]{:S(2)}) collective-permute-start(f32[2,256,512]{2,1,0:T(8,128)S(1)} %select_add_fusion.2), channel_id=1, source_target_pairs={{0,8},{8,16},{16,24},{1,9},{9,17},{17,25},{2,10},{10,18},{18,26},{... | collective-permute-start | bytes 3145736 | tf_op jit(solution)/shard_map/ppermute | solution.py:25
  (20 other events, 326.3 us)

commit v2 on v1

--- a/solution.py
+++ b/solution.py
@@ -148,36 +148,33 @@
     )(at, piece, probe_modes, measured, jnp.asarray(ahead), jnp.asarray(back))
 
 
-def summed(value, bits):
-    if not bits:
-        return value
-    axis, bit = bits[0]
-    upper = (lax.axis_index(axis) >> bit) & 1 == 1
+def token(*values):
+    bad = jnp.zeros((), jnp.bool_)
+    for value in values:
+        bad |= jnp.isnan(value[(0,) * value.ndim])
+    return bad.astype(jnp.int32)
+
+
+def halved(value, axis, bit, after=0):
+    upper = ((lax.axis_index(axis) + after) >> bit) & 1 == 1
     half = value.shape[0] // 2
     first, second = value[:half], value[half:]
     got = flipped(jnp.where(upper, first, second), axis, bit)
-    kept = jnp.where(upper, second, first) + got
-    rest = bits[1:]
-    if len(bits) == SPLIT_AT[0]:
-        quarter = half // 2
-        swapped = [rest[1], rest[0]] + rest[2:]
-        done = jnp.concatenate([summed(kept[:quarter], rest), summed(kept[quarter:], swapped)])
-    else:
-        done = summed(kept, rest)
-    other = flipped(done, axis, bit)
-    return jnp.concatenate([jnp.where(upper, other, done), jnp.where(upper, done, other)])
-
-
-SPLIT_AT = [0]
-
-
-def sum_all(value):
-    tx_bits = lax.axis_size("tx").bit_length() - 1
-    ty_bits = lax.axis_size("ty").bit_length() - 1
-    bits = [("tx", bit) for bit in range(tx_bits)] + [("ty", bit) for bit in reversed(range(ty_bits))]
-    SPLIT_AT[0] = len(bits)
-    flat = value.reshape(-1, value.shape[-1])
-    return summed(flat, bits).reshape(value.shape)
+    return jnp.where(upper, second, first) + got
+
+
+def doubled(value, axis, bit, after=0):
+    upper = ((lax.axis_index(axis) + after) >> bit) & 1 == 1
+    other = flipped(value, axis, bit)
+    return jnp.concatenate([jnp.where(upper, other, value), jnp.where(upper, value, other)])
+
+
+def summed_inner(value, bits):
+    for axis, bit in bits:
+        value = halved(value, axis, bit)
+    for axis, bit in reversed(bits):
+        value = doubled(value, axis, bit)
+    return value
 
 
 def local(specimen, probe_modes, amplitude, offsets, live_slots):
@@ -244,27 +241,53 @@
 
     works = [mine, theirs, before[0], before[1]]
     masks = [col_mask(work) for work in works]
-    tops, bottoms, aboves = [], [], []
+    terms = []
     for k in range(CHUNKS):
-        q = q_at(k)
         mine_k = grad[:, k * size : (k + 1) * size, :]
-        terms = [
+        terms.append([
             mine_k,
             flipped(mine_k, "tx", 0),
             lax.ppermute(mine_k, "tx", [(at, at + 2) for at in even_at]),
             lax.ppermute(mine_k, "tx", [(at + 1, at + 2) for at in even_at]),
+        ])
+
+    def placed(k, keep, after=0):
+        total = jnp.zeros((), jnp.float32)
+        for term, work, mask in zip(terms[k], works, masks):
+            total += jnp.where(mask & keep(q_at(k), work[0] + after), term, 0.0)
+        return total
+
+    def beyond(q, row):
+        return q + width < row
+
+    bits = [("tx", bit) for bit in range(1, n_tx.bit_length() - 1)]
+    swapped = [bits[1], bits[0]] + bits[2:]
+    deep = [("ty", bit) for bit in reversed(range(lax.axis_size("ty").bit_length() - 1))]
+    flat = mode_terms.reshape(-1, width)
+    kept = halved(flat, "tx", 0)
+    quarter = kept.shape[0] // 2
+    first_after = token(*terms[0][1:])
+    above_first = shifted(placed(0, beyond), "ty", 1)
+    sums = [
+        halved(part, *order[0], first_after)
+        for part, order in ((kept[:quarter], bits), (kept[quarter:], swapped))
+    ]
+    second_after = token(*terms[1][1:])
+    above_second = shifted(placed(1, beyond), "ty", 1)
+    sums = [
+        halved(part, *order[1], token(above_first) + second_after)
+        for part, order in zip(sums, (bits, swapped))
+    ]
+    sums = [summed_inner(part, order[2:] + deep) for part, order in zip(sums, (bits, swapped))]
+    last_after = token(above_second)
+    for at_bit in (1, 0):
+        sums = [
+            doubled(part, *order[at_bit], last_after) for part, order in zip(sums, (bits, swapped))
         ]
-        top = bottom = beyond = jnp.zeros((), jnp.float32)
-        for term, work, mask in zip(terms, works, masks):
-            row = work[0]
-            top += jnp.where(mask & (q >= row), term, 0.0)
-            bottom += jnp.where(mask & (q < row) & (q + width >= row), term, 0.0)
-            beyond += jnp.where(mask & (q + width < row), term, 0.0)
-        aboves.append(shifted(beyond, "ty", 1))
-        tops.append(top)
-        bottoms.append(bottom)
-    probe_grad = sum_all(mode_terms)
-    tops = [top + above for top, above in zip(tops, aboves)]
+    probe_grad = doubled(jnp.concatenate(sums), "tx", 0).reshape(mode_terms.shape)
+    aboves = [above_first, above_second]
+    tops = [placed(k, lambda q, row: q >= row) + aboves[k] for k in range(CHUNKS)]
+    bottoms = [placed(k, lambda q, row: (q < row) & (q + width >= row)) for k in range(CHUNKS)]
     return (jnp.concatenate(tops + bottoms, axis=1), probe_grad)
 
 

time: 360 us -> 385 us (1.069)
  waiting for transfers between devices: 200 us -> 166 us
  starting transfers between devices: 59.8 us -> 79.6 us
  other arithmetic: 56.5 us -> 73.9 us
  local copies, waits for them, and re-layouts: 5.25 us -> 15.4 us
  between operations: 10.6 us -> 20.4 us
    ppermute x4, waiting for transfers between devices: 61.3 us -> 29 us  [shifted(): lax.ppermute(value, axis, [(at, at + steps) for at in range(first, last)])]
    ppermute x2, waiting for transfers between devices: 49.2 us -> 18.5 us  [local(): lax.ppermute(picked(k, before[1]), 'tx', [(at + 2, at + 1) for at in even...]
    ppermute x24, starting transfers between devices: 31 us -> 58.7 us  [flipped(): lax.ppermute(value, axis, [(at, at ^ mask) for at in range(lax.axis_size(...]
    ppermute x24, waiting for transfers between devices: 68.6 us -> 96.1 us  [flipped(): lax.ppermute(value, axis, [(at, at ^ mask) for at in range(lax.axis_size(...]
    add x12, other arithmetic: 7.5 us -> 19.9 us  [the longest x2 7.34 us: local(): placed(k, lambda q, row: q >= row) + aboves[k]]
    ppermute x2, starting transfers between devices: 11.6 us -> 3.82 us  [local(): lax.ppermute(mine_k, 'tx', [(at + 1, at + 2) for at in even_at])]
    slice x0 -> x8, local copies, waits for them, and re-layouts: none -> 6.58 us  [token(): bad |= jnp.isnan(value[(0,) * value.ndim])]
    and x4 -> x10, other arithmetic: 3.79 us -> 8.76 us  [the longest x4 6.18 us: placed(): total += jnp.where(mask & keep(q_at(k), work[0] + after), term, 0.0)]
  transfers between devices with their start and end apart: 37 -> 37, of which waited for: 18 -> 22; matrix products, arithmetic and copies ran while one was open for 9% -> 15% of each run, Pallas kernels for 0% -> 0%
where the time goes in v2:
time: 385 us; the launch traced here: 382 us
  waiting for transfers between devices  166 us (43%)
  starting transfers between devices  79.6 us (21%)
  other arithmetic  73.9 us (19%)
  Pallas kernels  27.2 us (7%)
  between operations  20.4 us (5%)
  local copies, waits for them, and re-layouts  15.4 us (4%)
    ppermute x24, waiting for transfers between devices, flipped(): lax.ppermute(value, axis, [(at, at ^ mask) for at in range(lax.axis_size(...  96.1 us
    ppermute x24, starting transfers between devices, flipped(): lax.ppermute(value, axis, [(at, at ^ mask) for at in range(lax.axis_size(...  58.7 us
    ppermute x4, waiting for transfers between devices, shifted(): lax.ppermute(value, axis, [(at, at + steps) for at in range(first, last)])  29 us
    pallas_call x1, Pallas kernels, slot_terms(): pl.pallas_call(functools.partial(slot_kernel, scale), out_shape=(jax.Shap...  27.2 us
    ppermute x2, waiting for transfers between devices, local(): lax.ppermute(mine_k, 'tx', [(at + 1, at + 2) for at in even_at])  22.5 us
    ppermute x2, waiting for transfers between devices, local(): lax.ppermute(picked(k, before[1]), 'tx', [(at + 2, at + 1) for at in even...  18.5 us
    ppermute x4, starting transfers between devices, shifted(): lax.ppermute(value, axis, [(at, at + steps) for at in range(first, last)])  9.09 us
  transfers between devices with their start and end apart: 37, of which 22 were waited for; matrix products, arithmetic and copies ran while one was open for 15% of the time, Pallas kernels for 0%

profile of v2, /device:TPU:27, one launch (start us, length us, event | category | flops | bytes accessed | tf_op | source)
XLA Modules:
  0.0 382.5 jit_solution(2477623947782610054)
XLA Ops:
  19.3 10.8 %collective-permute-done.1 = f32[2,256,512]{2,1,0:T(8,128)S(1)} collective-permute-done((f32[2,256,512]{2,1,0:T(8,128)S(1)}, f32[2,256,512]{2,1,0:T(8,128)S(1)}, u32[]{:S(2)}, u32[]{:S(2)}) %collective-permute-start.1) | collective-permute-done | bytes 1048608 | tf_op jit(solution)/shard_map/ppermute | solution.py:25
  30.0 2.9 select_select_fusion.5
  38.4 11.8 %collective-permute-done.5 = f32[2,256,512]{2,1,0:T(8,128)} collective-permute-done((f32[2,256,512]{2,1,0:T(8,128)}, f32[2,256,512]{2,1,0:T(8,128)}, u32[]{:S(2)}, u32[]{:S(2)}) %collective-permute-start.5) | collective-permute-done | bytes 1048608 | tf_op jit(solution)/shard_map/ppermute | solution.py:224
  50.2 3.4 select_select_fusion.4
  53.7 4.2 %collective-permute-start.6 = (f32[2,256,512]{2,1,0:T(8,128)S(1)}, f32[2,256,512]{2,1,0:T(8,128)S(1)}, u32[]{:S(2)}, u32[]{:S(2)}) collective-permute-start(f32[2,256,512]{2,1,0:T(8,128)S(1)} %get-tuple-element.21), channel_id=1, source_target_pairs={{8,0},{16,8},{24,16},{9,1},{17,9},{25,17},{10,2},{18,10},{26,18},{... | collective-permute-start | bytes 3145736 | tf_op jit(solution)/shard_map/ppermute | solution.py:25
  58.9 12.2 %collective-permute-start.10 = (f32[512,512]{1,0:T(8,128)}, f32[512,512]{1,0:T(8,128)}, u32[]{:S(2)}, u32[]{:S(2)}) collective-permute-start(f32[512,512]{1,0:T(8,128)} %slice_bitcast_fusion), channel_id=1, source_target_pairs={{0,1},{1,0},{2,3},{3,2},{4,5},{5,4},{6,7},{7,6},{8,9},{9,8},{10,11... | collective-permute-start | bytes 3145736 | tf_op jit(solution)/shard_map/ppermute | solution.py:19
  73.7 3.2 select_select_fusion.1
  80.0 9.8 %collective-permute-start.7 = (f32[2,256,512]{2,1,0:T(8,128)S(1)}, f32[2,256,512]{2,1,0:T(8,128)}, u32[]{:S(2)}, u32[]{:S(2)}) collective-permute-start(f32[2,256,512]{2,1,0:T(8,128)S(1)} %get-tuple-element.19), channel_id=1, source_target_pairs={{0,1},{1,0},{2,3},{3,2},{4,5},{5,4},{6,7},{7,6},{8,9},{9,8},{10,11... | collective-permute-start | bytes 3145736 | tf_op jit(solution)/shard_map/ppermute | solution.py:19
  93.1 6.7 %collective-permute-done.9 = f32[2,256,512]{2,1,0:T(8,128)} collective-permute-done((f32[2,256,512]{2,1,0:T(8,128)}, f32[2,256,512]{2,1,0:T(8,128)}, u32[]{:S(2)}, u32[]{:S(2)}) %collective-permute-start.9) | collective-permute-done | bytes 1048608 | tf_op jit(solution)/shard_map/ppermute | solution.py:224
  99.8 2.9 select_select_fusion
  104.2 27.2 %shard_map.86 = (f32[2,512,512]{2,1,0:T(8,128)S(1)}, f32[2,3,512,512]{3,2,1,0:T(8,128)}) custom-call(s32[2]{0:T(128)S(1)} %pad_add_fusion.2.at_ref, f32[2,512,512]{2,1,0:T(8,128)} %pad_maximum_fusion.3.piece_ref, f32[2,3,512,512]{3,2,1,0:T(8,128)} %probe_ref.1, f32[512,512]{1,0:T(8,128)S(1)} %bitcast_select_fusion.amp_ref, ...), custom_call_target="tpu_custom_call" | custom-call | flops 12884901888 | bytes 25165824 | tf_op jit(solution)/shard_map/pallas_call | solution.py:130
  131.4 6.9 %slice_select_fusion.1 = (f32[1,3,512,512]{3,2,1,0:T(8,128)}, f32[1,3,512,512]{3,2,1,0:T(8,128)}) fusion(f32[2,3,512,512]{3,2,1,0:T(8,128)} %get-tuple-element.5, pred[]{:T(512)S(6)} %eq.82), kind=kLoop, calls=%fused_computation.5 | loop fusion | flops 1572864 | bytes 12582913 | tf_op jit(solution)/shard_map/jit(_where)/select_n | solution.py:163
  138.3 11.9 %collective-permute-start.19 = (f32[1536,512]{1,0:T(8,128)}, f32[1536,512]{1,0:T(8,128)}, u32[]{:S(2)}, u32[]{:S(2)}) collective-permute-start(f32[1536,512]{1,0:T(8,128)} %bitcast.32), channel_id=1, source_target_pairs={{0,1},{1,0},{2,3},{3,2},{4,5},{5,4},{6,7},{7,6},{8,9},{9,8},{10,11... | collective-permute-start | bytes 9437192 | tf_op jit(solution)/shard_map/ppermute | solution.py:19
  165.0 14.6 %collective-permute-done.13 = f32[2,256,512]{2,1,0:T(8,128)S(1)} collective-permute-done((f32[2,256,512]{2,1,0:T(8,128)S(1)}, f32[2,256,512]{2,1,0:T(8,128)S(1)}, u32[]{:S(2)}, u32[]{:S(2)}) %collective-permute-start.13) | collective-permute-done | bytes 1048608 | tf_op jit(solution)/shard_map/ppermute | solution.py:251
  179.6 2.6 select_add_fusion.3
  189.0 18.2 %collective-permute-done.14 = f32[2,256,512]{2,1,0:T(8,128)} collective-permute-done((f32[2,256,512]{2,1,0:T(8,128)}, f32[2,256,512]{2,1,0:T(8,128)}, u32[]{:S(2)}, u32[]{:S(2)}) %collective-permute-start.14) | collective-permute-done | bytes 1048608 | tf_op jit(solution)/shard_map/ppermute | solution.py:25
  207.2 4.8 %add_add_fusion.1 = (f32[2,256,512]{2,1,0:T(8,128)}, f32[2,256,512]{2,1,0:T(8,128)}, f32[2,256,512]{2,1,0:T(8,128)}) fusion(f32[2,256,512]{2,1,0:T(8,128)} %collective-permute-done.14, f32[2,256,512]{2,1,0:T(8,128)} %copy-done.4, f32[2,256,512]{2,1,0:T(8,128)S(1)} %collective-permute-done.12, f32[2,256,512]{2,1,0:T(8,128)} %copy-done.3, ...), kind=kLoop, calls=%fused_computation.15 | loop fusion | flops 3932160 | bytes 10485760 | tf_op jit(solution)/shard_map/add | solution.py:289
  212.8 4.8 %collective-permute-start.15 = (f32[2,256,512]{2,1,0:T(8,128)}, f32[2,256,512]{2,1,0:T(8,128)}, u32[]{:S(2)}, u32[]{:S(2)}) collective-permute-start(f32[2,256,512]{2,1,0:T(8,128)} %get-tuple-element.26), channel_id=1, source_target_pairs={{0,1},{1,0},{2,3},{3,2},{4,5},{5,4},{6,7},{7,6},{8,9},{9,8},{10,11... | collective-permute-start | bytes 3145736 | tf_op jit(solution)/shard_map/ppermute | solution.py:19
  234.3 7.9 %collective-permute-done.17 = f32[2,256,512]{2,1,0:T(8,128)} collective-permute-done((f32[2,256,512]{2,1,0:T(8,128)}, f32[2,256,512]{2,1,0:T(8,128)}, u32[]{:S(2)}, u32[]{:S(2)}) %collective-permute-start.17) | collective-permute-done | bytes 1048608 | tf_op jit(solution)/shard_map/ppermute | solution.py:251
  244.6 15.4 %collective-permute-done.20 = f32[384,512]{1,0:T(8,128)} collective-permute-done((f32[384,512]{1,0:T(8,128)}, f32[384,512]{1,0:T(8,128)}, u32[]{:S(2)}, u32[]{:S(2)}) %collective-permute-start.20) | collective-permute-done | bytes 786464 | tf_op jit(solution)/shard_map/ppermute | solution.py:19
  260.0 3.0 select_add_fusion.5
  264.7 3.1 select_add_fusion.2
  270.6 5.1 %collective-permute-done.29 = f32[192,512]{1,0:T(8,128)} collective-permute-done((f32[192,512]{1,0:T(8,128)}, f32[192,512]{1,0:T(8,128)}, u32[]{:S(2)}, u32[]{:S(2)}) %collective-permute-start.29) | collective-permute-done | bytes 393248 | tf_op jit(solution)/shard_map/ppermute | solution.py:19
  280.3 3.0 collective-permute-start.22
  283.3 25.5 %collective-permute-done.30 = f32[96,512]{1,0:T(8,128)S(1)} collective-permute-done((f32[96,512]{1,0:T(8,128)S(1)}, f32[96,512]{1,0:T(8,128)S(1)}, u32[]{:S(2)}, u32[]{:S(2)}) %collective-permute-start.30) | collective-permute-done | bytes 196640 | tf_op jit(solution)/shard_map/ppermute | solution.py:19
  309.0 4.1 %collective-permute-done.22 = f32[96,512]{1,0:T(8,128)S(1)} collective-permute-done((f32[96,512]{1,0:T(8,128)S(1)}, f32[96,512]{1,0:T(8,128)S(1)}, u32[]{:S(2)}, u32[]{:S(2)}) %collective-permute-start.22) | collective-permute-done | bytes 196640 | tf_op jit(solution)/shard_map/ppermute | solution.py:19
  321.8 13.5 %collective-permute-done.33 = f32[96,512]{1,0:T(8,128)S(1)} collective-permute-done((f32[96,512]{1,0:T(8,128)S(1)}, f32[96,512]{1,0:T(8,128)S(1)}, u32[]{:S(2)}, u32[]{:S(2)}) %collective-permute-start.33) | collective-permute-done | bytes 196640 | tf_op jit(solution)/shard_map/ppermute | solution.py:19
  343.4 3.2 collective-permute-done.34
  347.8 3.1 collective-permute-done.26
  353.5 14.1 %collective-permute-done.35 = f32[384,512]{1,0:T(8,128)S(1)} collective-permute-done((f32[384,512]{1,0:T(8,128)S(1)}, f32[384,512]{1,0:T(8,128)S(1)}, u32[]{:S(2)}, u32[]{:S(2)}) %collective-permute-start.35) | collective-permute-done | bytes 786464 | tf_op jit(solution)/shard_map/ppermute | solution.py:19
  369.4 3.3 collective-permute-start.36
  379.0 3.4 pad_maximum_fusion
  (206 shorter events, 95.6 us)
Async XLA Ops:
  5.4 24.6 %collective-permute-start.1 = (f32[2,256,512]{2,1,0:T(8,128)S(1)}, f32[2,256,512]{2,1,0:T(8,128)S(1)}, u32[]{:S(2)}, u32[]{:S(2)}) collective-permute-start(f32[2,256,512]{2,1,0:T(8,128)S(1)} %slice.214), channel_id=1, source_target_pairs={{8,0},{16,8},{24,16},{9,1},{17,9},{25,17},{10,2},{18,10},{26,18},{... | collective-permute-start | bytes 3145736 | tf_op jit(solution)/shard_map/ppermute | solution.py:25
  32.9 17.3 %collective-permute-start.5 = (f32[2,256,512]{2,1,0:T(8,128)}, f32[2,256,512]{2,1,0:T(8,128)}, u32[]{:S(2)}, u32[]{:S(2)}) collective-permute-start(f32[2,256,512]{2,1,0:T(8,128)} %get-tuple-element.14), channel_id=1, source_target_pairs={{2,1},{4,3},{6,5},{10,9},{12,11},{14,13},{18,17},{20,19},{22,21},{... | collective-permute-start | bytes 3145736 | tf_op jit(solution)/shard_map/ppermute | solution.py:224
  34.2 16.0 %collective-permute-start.4 = (f32[2,256,512]{2,1,0:T(8,128)S(1)}, f32[2,256,512]{2,1,0:T(8,128)}, u32[]{:S(2)}, u32[]{:S(2)}) collective-permute-start(f32[2,256,512]{2,1,0:T(8,128)S(1)} %get-tuple-element.15), channel_id=1, source_target_pairs={{2,0},{4,2},{6,4},{10,8},{12,10},{14,12},{18,16},{20,18},{22,20},{... | collective-permute-start | bytes 3145736 | tf_op jit(solution)/shard_map/ppermute | solution.py:223
  35.8 14.4 %collective-permute-start.2 = (f32[2,256,512]{2,1,0:T(8,128)S(1)}, f32[2,256,512]{2,1,0:T(8,128)}, u32[]{:S(2)}, u32[]{:S(2)}) collective-permute-start(f32[2,256,512]{2,1,0:T(8,128)S(1)} %get-tuple-element.16), channel_id=1, source_target_pairs={{0,1},{1,0},{2,3},{3,2},{4,5},{5,4},{6,7},{7,6},{8,9},{9,8},{10,11... | collective-permute-start | bytes 3145736 | tf_op jit(solution)/shard_map/ppermute | solution.py:19
  53.7 20.1 %collective-permute-start.6 = (f32[2,256,512]{2,1,0:T(8,128)S(1)}, f32[2,256,512]{2,1,0:T(8,128)S(1)}, u32[]{:S(2)}, u32[]{:S(2)}) collective-permute-start(f32[2,256,512]{2,1,0:T(8,128)S(1)} %get-tuple-element.21), channel_id=1, source_target_pairs={{8,0},{16,8},{24,16},{9,1},{17,9},{25,17},{10,2},{18,10},{26,18},{... | collective-permute-start | bytes 3145736 | tf_op jit(solution)/shard_map/ppermute | solution.py:25
  58.9 32.8 %collective-permute-start.10 = (f32[512,512]{1,0:T(8,128)}, f32[512,512]{1,0:T(8,128)}, u32[]{:S(2)}, u32[]{:S(2)}) collective-permute-start(f32[512,512]{1,0:T(8,128)} %slice_bitcast_fusion), channel_id=1, source_target_pairs={{0,1},{1,0},{2,3},{3,2},{4,5},{5,4},{6,7},{7,6},{8,9},{9,8},{10,11... | collective-permute-start | bytes 3145736 | tf_op jit(solution)/shard_map/ppermute | solution.py:19
  77.0 22.8 %collective-permute-start.9 = (f32[2,256,512]{2,1,0:T(8,128)}, f32[2,256,512]{2,1,0:T(8,128)}, u32[]{:S(2)}, u32[]{:S(2)}) collective-permute-start(f32[2,256,512]{2,1,0:T(8,128)} %get-tuple-element.17), channel_id=1, source_target_pairs={{2,1},{4,3},{6,5},{10,9},{12,11},{14,13},{18,17},{20,19},{22,21},{... | collective-permute-start | bytes 3145736 | tf_op jit(solution)/shard_map/ppermute | solution.py:224
  78.3 21.5 %collective-permute-start.8 = (f32[2,256,512]{2,1,0:T(8,128)}, f32[2,256,512]{2,1,0:T(8,128)}, u32[]{:S(2)}, u32[]{:S(2)}) collective-permute-start(f32[2,256,512]{2,1,0:T(8,128)} %get-tuple-element.18), channel_id=1, source_target_pairs={{2,0},{4,2},{6,4},{10,8},{12,10},{14,12},{18,16},{20,18},{22,20},{... | collective-permute-start | bytes 3145736 | tf_op jit(solution)/shard_map/ppermute | solution.py:223
  80.0 19.8 %collective-permute-start.7 = (f32[2,256,512]{2,1,0:T(8,128)S(1)}, f32[2,256,512]{2,1,0:T(8,128)}, u32[]{:S(2)}, u32[]{:S(2)}) collective-permute-start(f32[2,256,512]{2,1,0:T(8,128)S(1)} %get-tuple-element.19), channel_id=1, source_target_pairs={{0,1},{1,0},{2,3},{3,2},{4,5},{5,4},{6,7},{7,6},{8,9},{9,8},{10,11... | collective-permute-start | bytes 3145736 | tf_op jit(solution)/shard_map/ppermute | solution.py:19
  138.3 81.6 %collective-permute-start.19 = (f32[1536,512]{1,0:T(8,128)}, f32[1536,512]{1,0:T(8,128)}, u32[]{:S(2)}, u32[]{:S(2)}) collective-permute-start(f32[1536,512]{1,0:T(8,128)} %bitcast.32), channel_id=1, source_target_pairs={{0,1},{1,0},{2,3},{3,2},{4,5},{5,4},{6,7},{7,6},{8,9},{9,8},{10,11... | collective-permute-start | bytes 9437192 | tf_op jit(solution)/shard_map/ppermute | solution.py:19
  154.5 10.5 %collective-permute-start.12 = (f32[2,256,512]{2,1,0:T(8,128)S(1)}, f32[2,256,512]{2,1,0:T(8,128)S(1)}, u32[]{:S(2)}, u32[]{:S(2)}) collective-permute-start(f32[2,256,512]{2,1,0:T(8,128)S(1)} %slice.227), channel_id=1, source_target_pairs={{0,2},{2,4},{4,6},{8,10},{10,12},{12,14},{16,18},{18,20},{20,22},{... | collective-permute-start | bytes 3145736 | tf_op jit(solution)/shard_map/ppermute | solution.py:250
  155.3 9.8 %collective-permute-start.11 = (f32[2,256,512]{2,1,0:T(8,128)S(1)}, f32[2,256,512]{2,1,0:T(8,128)S(1)}, u32[]{:S(2)}, u32[]{:S(2)}) collective-permute-start(f32[2,256,512]{2,1,0:T(8,128)S(1)} %slice.227), channel_id=1, source_target_pairs={{0,1},{1,0},{2,3},{3,2},{4,5},{5,4},{6,7},{7,6},{8,9},{9,8},{10,11... | collective-permute-start | bytes 3145736 | tf_op jit(solution)/shard_map/ppermute | solution.py:19
  156.5 23.1 %collective-permute-start.13 = (f32[2,256,512]{2,1,0:T(8,128)S(1)}, f32[2,256,512]{2,1,0:T(8,128)S(1)}, u32[]{:S(2)}, u32[]{:S(2)}) collective-permute-start(f32[2,256,512]{2,1,0:T(8,128)S(1)} %slice.227), channel_id=1, source_target_pairs={{1,2},{3,4},{5,6},{9,10},{11,12},{13,14},{17,18},{19,20},{21,22},{... | collective-permute-start | bytes 3145736 | tf_op jit(solution)/shard_map/ppermute | solution.py:251
  182.2 25.0 %collective-permute-start.14 = (f32[2,256,512]{2,1,0:T(8,128)}, f32[2,256,512]{2,1,0:T(8,128)}, u32[]{:S(2)}, u32[]{:S(2)}) collective-permute-start(f32[2,256,512]{2,1,0:T(8,128)} %select_add_fusion.3), channel_id=1, source_target_pairs={{0,8},{8,16},{16,24},{1,9},{9,17},{17,25},{2,10},{10,18},{18,26},{... | collective-permute-start | bytes 3145736 | tf_op jit(solution)/shard_map/ppermute | solution.py:25
  212.1 17.8 %collective-permute-start.16 = (f32[2,256,512]{2,1,0:T(8,128)}, f32[2,256,512]{2,1,0:T(8,128)S(1)}, u32[]{:S(2)}, u32[]{:S(2)}) collective-permute-start(f32[2,256,512]{2,1,0:T(8,128)} %get-tuple-element.26), channel_id=1, source_target_pairs={{0,2},{2,4},{4,6},{8,10},{10,12},{12,14},{16,18},{18,20},{20,22},{... | collective-permute-start | bytes 3145736 | tf_op jit(solution)/shard_map/ppermute | solution.py:250
  212.8 19.0 %collective-permute-start.15 = (f32[2,256,512]{2,1,0:T(8,128)}, f32[2,256,512]{2,1,0:T(8,128)}, u32[]{:S(2)}, u32[]{:S(2)}) collective-permute-start(f32[2,256,512]{2,1,0:T(8,128)} %get-tuple-element.26), channel_id=1, source_target_pairs={{0,1},{1,0},{2,3},{3,2},{4,5},{5,4},{6,7},{7,6},{8,9},{9,8},{10,11... | collective-permute-start | bytes 3145736 | tf_op jit(solution)/shard_map/ppermute | solution.py:19
  217.6 24.6 %collective-permute-start.17 = (f32[2,256,512]{2,1,0:T(8,128)}, f32[2,256,512]{2,1,0:T(8,128)}, u32[]{:S(2)}, u32[]{:S(2)}) collective-permute-start(f32[2,256,512]{2,1,0:T(8,128)} %get-tuple-element.26), channel_id=1, source_target_pairs={{1,2},{3,4},{5,6},{9,10},{11,12},{13,14},{17,18},{19,20},{21,22},{... | collective-permute-start | bytes 3145736 | tf_op jit(solution)/shard_map/ppermute | solution.py:251
  225.3 34.6 %collective-permute-start.20 = (f32[384,512]{1,0:T(8,128)}, f32[384,512]{1,0:T(8,128)}, u32[]{:S(2)}, u32[]{:S(2)}) collective-permute-start(f32[384,512]{1,0:T(8,128)} %get-tuple-element.24), channel_id=1, source_target_pairs={{0,2},{1,3},{2,0},{3,1},{4,6},{5,7},{6,4},{7,5},{8,10},{9,11},{10,... | collective-permute-start | bytes 2359304 | tf_op jit(solution)/shard_map/ppermute | solution.py:19
  227.3 32.7 %collective-permute-start.28 = (f32[384,512]{1,0:T(8,128)}, f32[384,512]{1,0:T(8,128)}, u32[]{:S(2)}, u32[]{:S(2)}) collective-permute-start(f32[384,512]{1,0:T(8,128)} %get-tuple-element.25), channel_id=1, source_target_pairs={{0,4},{1,5},{2,6},{3,7},{4,0},{5,1},{6,2},{7,3},{8,12},{9,13},{10,... | collective-permute-start | bytes 2359304 | tf_op jit(solution)/shard_map/ppermute | solution.py:19
  264.6 11.0 %collective-permute-start.29 = (f32[192,512]{1,0:T(8,128)}, f32[192,512]{1,0:T(8,128)}, u32[]{:S(2)}, u32[]{:S(2)}) collective-permute-start(f32[192,512]{1,0:T(8,128)} %slice_select_fusion.4), channel_id=1, source_target_pairs={{0,2},{1,3},{2,0},{3,1},{4,6},{5,7},{6,4},{7,5},{8,10},{9,11},{10,... | collective-permute-start | bytes 1179656 | tf_op jit(solution)/shard_map/ppermute | solution.py:19
  267.8 72.6 %collective-permute-start.18 = (f32[2,256,512]{2,1,0:T(8,128)}, f32[2,256,512]{2,1,0:T(8,128)S(1)}, u32[]{:S(2)}, u32[]{:S(2)}) collective-permute-start(f32[2,256,512]{2,1,0:T(8,128)} %select_add_fusion.2), channel_id=1, source_target_pairs={{0,8},{8,16},{16,24},{1,9},{9,17},{17,25},{2,10},{10,18},{18,26},{... | collective-permute-start | bytes 3145736 | tf_op jit(solution)/shard_map/ppermute | solution.py:25
  269.4 10.8 %collective-permute-start.21 = (f32[192,512]{1,0:T(8,128)S(1)}, f32[192,512]{1,0:T(8,128)S(1)}, u32[]{:S(2)}, u32[]{:S(2)}) collective-permute-start(f32[192,512]{1,0:T(8,128)S(1)} %slice_select_fusion.5), channel_id=1, source_target_pairs={{0,4},{1,5},{2,6},{3,7},{4,0},{5,1},{6,2},{7,3},{8,12},{9,13},{10,... | collective-permute-start | bytes 1179656 | tf_op jit(solution)/shard_map/ppermute | solution.py:19
  277.0 31.8 %collective-permute-start.30 = (f32[96,512]{1,0:T(8,128)S(1)}, f32[96,512]{1,0:T(8,128)S(1)}, u32[]{:S(2)}, u32[]{:S(2)}) collective-permute-start(f32[96,512]{1,0:T(8,128)S(1)} %slice_select_fusion.6), channel_id=1, source_target_pairs={{0,16},{8,24},{16,0},{24,8},{1,17},{9,25},{17,1},{25,9},{2,18},{10... | collective-permute-start | bytes 589832 | tf_op jit(solution)/shard_map/ppermute | solution.py:19
  280.3 32.8 %collective-permute-start.22 = (f32[96,512]{1,0:T(8,128)S(1)}, f32[96,512]{1,0:T(8,128)S(1)}, u32[]{:S(2)}, u32[]{:S(2)}) collective-permute-start(f32[96,512]{1,0:T(8,128)S(1)} %slice_select_fusion.7), channel_id=1, source_target_pairs={{0,16},{8,24},{16,0},{24,8},{1,17},{9,25},{17,1},{25,9},{2,18},{10... | collective-permute-start | bytes 589832 | tf_op jit(solution)/shard_map/ppermute | solution.py:19
  308.9 6.2 %collective-permute-start.31 = (f32[48,512]{1,0:T(8,128)S(1)}, f32[48,512]{1,0:T(8,128)S(1)}, u32[]{:S(2)}, u32[]{:S(2)}) collective-permute-start(f32[48,512]{1,0:T(8,128)S(1)} %slice_select_fusion.8), channel_id=1, source_target_pairs={{0,8},{8,0},{16,24},{24,16},{1,9},{9,1},{17,25},{25,17},{2,10},{10... | collective-permute-start | bytes 294920 | tf_op jit(solution)/shard_map/ppermute | solution.py:19
  319.3 16.1 %collective-permute-start.33 = (f32[96,512]{1,0:T(8,128)S(1)}, f32[96,512]{1,0:T(8,128)S(1)}, u32[]{:S(2)}, u32[]{:S(2)}) collective-permute-start(f32[96,512]{1,0:T(8,128)S(1)} %pad_maximum_fusion.9), channel_id=1, source_target_pairs={{0,16},{8,24},{16,0},{24,8},{1,17},{9,25},{17,1},{25,9},{2,18},{10... | collective-permute-start | bytes 589832 | tf_op jit(solution)/shard_map/ppermute | solution.py:19
  320.9 18.7 %collective-permute-start.25 = (f32[96,512]{1,0:T(8,128)S(1)}, f32[96,512]{1,0:T(8,128)S(1)}, u32[]{:S(2)}, u32[]{:S(2)}) collective-permute-start(f32[96,512]{1,0:T(8,128)S(1)} %pad_maximum_fusion.8), channel_id=1, source_target_pairs={{0,16},{8,24},{16,0},{24,8},{1,17},{9,25},{17,1},{25,9},{2,18},{10... | collective-permute-start | bytes 589832 | tf_op jit(solution)/shard_map/ppermute | solution.py:19
  336.2 10.4 %collective-permute-start.34 = (f32[192,512]{1,0:T(8,128)}, f32[192,512]{1,0:T(8,128)}, u32[]{:S(2)}, u32[]{:S(2)}) collective-permute-start(f32[192,512]{1,0:T(8,128)} %pad_maximum_fusion.7), channel_id=1, source_target_pairs={{0,2},{1,3},{2,0},{3,1},{4,6},{5,7},{6,4},{7,5},{8,10},{9,11},{10,... | collective-permute-start | bytes 1179656 | tf_op jit(solution)/shard_map/ppermute | solution.py:19
  340.4 10.5 %collective-permute-start.26 = (f32[192,512]{1,0:T(8,128)}, f32[192,512]{1,0:T(8,128)}, u32[]{:S(2)}, u32[]{:S(2)}) collective-permute-start(f32[192,512]{1,0:T(8,128)} %pad_maximum_fusion.6), channel_id=1, source_target_pairs={{0,4},{1,5},{2,6},{3,7},{4,0},{5,1},{6,2},{7,3},{8,12},{9,13},{10,... | collective-permute-start | bytes 1179656 | tf_op jit(solution)/shard_map/ppermute | solution.py:19
  347.7 19.9 %collective-permute-start.35 = (f32[384,512]{1,0:T(8,128)S(1)}, f32[384,512]{1,0:T(8,128)S(1)}, u32[]{:S(2)}, u32[]{:S(2)}) collective-permute-start(f32[384,512]{1,0:T(8,128)S(1)} %pad_maximum_fusion.5), channel_id=1, source_target_pairs={{0,4},{1,5},{2,6},{3,7},{4,0},{5,1},{6,2},{7,3},{8,12},{9,13},{10,... | collective-permute-start | bytes 2359304 | tf_op jit(solution)/shard_map/ppermute | solution.py:19
  352.0 16.8 %collective-permute-start.27 = (f32[384,512]{1,0:T(8,128)S(1)}, f32[384,512]{1,0:T(8,128)S(1)}, u32[]{:S(2)}, u32[]{:S(2)}) collective-permute-start(f32[384,512]{1,0:T(8,128)S(1)} %pad_maximum_fusion.4), channel_id=1, source_target_pairs={{0,2},{1,3},{2,0},{3,1},{4,6},{5,7},{6,4},{7,5},{8,10},{9,11},{10,... | collective-permute-start | bytes 2359304 | tf_op jit(solution)/shard_map/ppermute | solution.py:19
  369.4 8.6 %collective-permute-start.36 = (f32[1536,512]{1,0:T(8,128)S(1)}, f32[1536,512]{1,0:T(8,128)S(1)}, u32[]{:S(2)}, u32[]{:S(2)}) collective-permute-start(f32[1536,512]{1,0:T(8,128)S(1)} %pad_maximum_fusion.2), channel_id=1, source_target_pairs={{0,1},{1,0},{2,3},{3,2},{4,5},{5,4},{6,7},{7,6},{8,9},{9,8},{10,11... | collective-permute-start | bytes 9437192 | tf_op jit(solution)/shard_map/ppermute | solution.py:19
  (41 other events, 398.0 us)

commit v3 on v2

--- a/solution.py
+++ b/solution.py
@@ -10,7 +10,7 @@
 from jax.experimental.pallas import tpu as pltpu
 from jax.sharding import PartitionSpec as P
 
-CHUNKS = 2
+CHUNKS = 1
 ROWS = 32
 
 
@@ -266,27 +266,23 @@
     flat = mode_terms.reshape(-1, width)
     kept = halved(flat, "tx", 0)
     quarter = kept.shape[0] // 2
-    first_after = token(*terms[0][1:])
-    above_first = shifted(placed(0, beyond), "ty", 1)
     sums = [
-        halved(part, *order[0], first_after)
+        halved(part, *order[0])
         for part, order in ((kept[:quarter], bits), (kept[quarter:], swapped))
     ]
-    second_after = token(*terms[1][1:])
-    above_second = shifted(placed(1, beyond), "ty", 1)
+    aside_after = token(*terms[0][1:])
+    above = shifted(placed(0, beyond), "ty", 1)
     sums = [
-        halved(part, *order[1], token(above_first) + second_after)
-        for part, order in zip(sums, (bits, swapped))
+        halved(part, *order[1], aside_after) for part, order in zip(sums, (bits, swapped))
     ]
     sums = [summed_inner(part, order[2:] + deep) for part, order in zip(sums, (bits, swapped))]
-    last_after = token(above_second)
+    last_after = token(above)
     for at_bit in (1, 0):
         sums = [
             doubled(part, *order[at_bit], last_after) for part, order in zip(sums, (bits, swapped))
         ]
     probe_grad = doubled(jnp.concatenate(sums), "tx", 0).reshape(mode_terms.shape)
-    aboves = [above_first, above_second]
-    tops = [placed(k, lambda q, row: q >= row) + aboves[k] for k in range(CHUNKS)]
+    tops = [placed(k, lambda q, row: q >= row) + above for k in range(CHUNKS)]
     bottoms = [placed(k, lambda q, row: (q < row) & (q + width >= row)) for k in range(CHUNKS)]
     return (jnp.concatenate(tops + bottoms, axis=1), probe_grad)
 

time: 385 us -> 364 us (0.945)
  starting transfers between devices: 79.6 us -> 62.4 us
  waiting for transfers between devices: 166 us -> 183 us
  other arithmetic: 73.9 us -> 61.4 us
  between operations: 20.4 us -> 15 us
    ppermute x24 -> x22, waiting for transfers between devices: 96.1 us -> 113 us  [flipped(): lax.ppermute(value, axis, [(at, at ^ mask) for at in range(lax.axis_size(...]
    ppermute x24 -> x22, starting transfers between devices: 58.7 us -> 49.2 us  [flipped(): lax.ppermute(value, axis, [(at, at ^ mask) for at in range(lax.axis_size(...]
    ppermute x4 -> x2, starting transfers between devices: 9.09 us -> 3.47 us  [shifted(): lax.ppermute(value, axis, [(at, at + steps) for at in range(first, last)])]
    ppermute x2 -> x1, waiting for transfers between devices: 18.5 us -> 15.4 us  [local(): lax.ppermute(picked(k, before[1]), 'tx', [(at + 2, at + 1) for at in even...]
    ppermute x2 -> x1, waiting for transfers between devices: 22.5 us -> 24.9 us  [local(): lax.ppermute(mine_k, 'tx', [(at + 1, at + 2) for at in even_at])]
    ppermute x4 -> x2, waiting for transfers between devices: 29 us -> 30.3 us  [shifted(): lax.ppermute(value, axis, [(at, at + steps) for at in range(first, last)])]
  transfers between devices with their start and end apart: 37 -> 29, of which waited for: 22 -> 18; matrix products, arithmetic and copies ran while one was open for 15% -> 12% of each run, Pallas kernels for 0% -> 0%
where the time goes in v3:
time: 364 us; the launch traced here: 362 us
  waiting for transfers between devices  183 us (50%)
  starting transfers between devices  62.4 us (17%)
  other arithmetic  61.4 us (17%)
  Pallas kernels  27.2 us (7%)
  between operations  15 us (4%)
  local copies, waits for them, and re-layouts  12.9 us (4%)
    ppermute x22, waiting for transfers between devices, flipped(): lax.ppermute(value, axis, [(at, at ^ mask) for at in range(lax.axis_size(...  113 us
    ppermute x22, starting transfers between devices, flipped(): lax.ppermute(value, axis, [(at, at ^ mask) for at in range(lax.axis_size(...  49.2 us
    ppermute x2, waiting for transfers between devices, shifted(): lax.ppermute(value, axis, [(at, at + steps) for at in range(first, last)])  30.3 us
    pallas_call x1, Pallas kernels, slot_terms(): pl.pallas_call(functools.partial(slot_kernel, scale), out_shape=(jax.Shap...  27.2 us
    ppermute x1, waiting for transfers between devices, local(): lax.ppermute(mine_k, 'tx', [(at + 1, at + 2) for at in even_at])  24.9 us
    ppermute x1, waiting for transfers between devices, local(): lax.ppermute(picked(k, before[1]), 'tx', [(at + 2, at + 1) for at in even...  15.4 us
    add x8, other arithmetic, halved(): return jnp.where(upper, second, first) + got  8.04 us
  transfers between devices with their start and end apart: 29, of which 18 were waited for; matrix products, arithmetic and copies ran while one was open for 12% of the time, Pallas kernels for 0%

profile of v3, /device:TPU:27, one launch (start us, length us, event | category | flops | bytes accessed | tf_op | source)
XLA Modules:
  0.0 362.3 jit_solution(1240153473852782689)
XLA Ops:
  0.6 3.1 slice.170
  20.1 30.3 %collective-permute-done.1 = f32[2,512,512]{2,1,0:T(8,128)S(1)} collective-permute-done((f32[2,512,512]{2,1,0:T(8,128)}, f32[2,512,512]{2,1,0:T(8,128)S(1)}, u32[]{:S(2)}, u32[]{:S(2)}) %collective-permute-start.1) | collective-permute-done | bytes 2097184 | tf_op jit(solution)/shard_map/ppermute | solution.py:25
  50.4 4.8 %select_select_fusion.1 = (f32[2,512,512]{2,1,0:T(8,128)}, f32[2,512,512]{2,1,0:T(8,128)}, f32[2,512,512]{2,1,0:T(8,128)}) fusion(f32[2,512,512]{2,1,0:T(8,128)S(1)} %collective-permute-done.1, f32[2,1024,512]{2,1,0:T(8,128)} %param.7, pred[512]{0:T(512)(128)(4,1)S(1)} %iota_compare_fusion.10, pred[512]{0:T(512)(128)(4,1)S(1)} %fusion.4, ...), kind=kLoop, calls=%fused_computation.10 | loop fusion | flops 3145728 | bytes 12585984 | tf_op jit(solution)/shard_map/jit(_where)/select_n | solution.py:219
  58.5 2.9 collective-permute-start.2
  62.5 4.3 %collective-permute-done.6 = f32[512,512]{1,0:T(8,128)S(1)} collective-permute-done((f32[512,512]{1,0:T(8,128)}, f32[512,512]{1,0:T(8,128)S(1)}, u32[]{:S(2)}, u32[]{:S(2)}) %collective-permute-start.6) | collective-permute-done | bytes 1048608 | tf_op jit(solution)/shard_map/ppermute | solution.py:19
  68.3 15.4 %collective-permute-done.5 = f32[2,512,512]{2,1,0:T(8,128)} collective-permute-done((f32[2,512,512]{2,1,0:T(8,128)}, f32[2,512,512]{2,1,0:T(8,128)}, u32[]{:S(2)}, u32[]{:S(2)}) %collective-permute-start.5) | collective-permute-done | bytes 2097184 | tf_op jit(solution)/shard_map/ppermute | solution.py:224
  83.7 5.6 %select_select_fusion.piece_ref = f32[2,512,512]{2,1,0:T(8,128)} fusion(f32[2,512,512]{2,1,0:T(8,128)} %collective-permute-done.2, f32[2,512,512]{2,1,0:T(8,128)} %collective-permute-done.4, f32[2,512,512]{2,1,0:T(8,128)} %collective-permute-done.5, f32[2,512,512]{2,1,0:T(8,128)S(1)} %collective-permute-done.1, f32[2,1024,512]{2,1,0:T(8,128)} %param.7, ...), kind=kLoop, calls=%fused_computation.9 | loop fusion | flops 4194304 | bytes 14681604 | tf_op jit(solution)/shard_map/jit(_where)/select_n | solution.py:232
  89.4 27.2 %shard_map.86 = (f32[2,512,512]{2,1,0:T(8,128)S(1)}, f32[2,3,512,512]{3,2,1,0:T(8,128)}) custom-call(s32[2]{0:T(128)S(1)} %pad_add_fusion.2.at_ref, f32[2,512,512]{2,1,0:T(8,128)} %select_select_fusion.piece_ref, f32[2,3,512,512]{3,2,1,0:T(8,128)} %probe_ref.1, f32[512,512]{1,0:T(8,128)S(1)} %bitcast_select_fusion.amp_ref, ...), custom_call_target="tpu_custom_call" | custom-call | flops 12884901888 | bytes 25165824 | tf_op jit(solution)/shard_map/pallas_call | solution.py:130
  116.5 6.9 %slice_select_fusion.1 = (f32[1,3,512,512]{3,2,1,0:T(8,128)}, f32[1,3,512,512]{3,2,1,0:T(8,128)}) fusion(f32[2,3,512,512]{3,2,1,0:T(8,128)} %get-tuple-element.5, pred[]{:T(512)S(6)} %eq.78), kind=kLoop, calls=%fused_computation.5 | loop fusion | flops 1572864 | bytes 12582913 | tf_op jit(solution)/shard_map/jit(_where)/select_n | solution.py:163
  123.4 23.2 %collective-permute-start.11 = (f32[1536,512]{1,0:T(8,128)}, f32[1536,512]{1,0:T(8,128)}, u32[]{:S(2)}, u32[]{:S(2)}) collective-permute-start(f32[1536,512]{1,0:T(8,128)} %bitcast.31), channel_id=1, source_target_pairs={{0,1},{1,0},{2,3},{3,2},{4,5},{5,4},{6,7},{7,6},{8,9},{9,8},{10,11... | collective-permute-start | bytes 9437192 | tf_op jit(solution)/shard_map/ppermute | solution.py:19
  147.6 3.8 %collective-permute-start.9 = (f32[2,512,512]{2,1,0:T(8,128)S(1)}, f32[2,512,512]{2,1,0:T(8,128)}, u32[]{:S(2)}, u32[]{:S(2)}) collective-permute-start(f32[2,512,512]{2,1,0:T(8,128)S(1)} %get-tuple-element.4), channel_id=1, source_target_pairs={{1,2},{3,4},{5,6},{9,10},{11,12},{13,14},{17,18},{19,20},{21,22},{... | collective-permute-start | bytes 6291464 | tf_op jit(solution)/shard_map/ppermute | solution.py:251
  157.8 3.6 bitcast_add_fusion
  168.7 24.9 %collective-permute-done.9 = f32[2,512,512]{2,1,0:T(8,128)} collective-permute-done((f32[2,512,512]{2,1,0:T(8,128)S(1)}, f32[2,512,512]{2,1,0:T(8,128)}, u32[]{:S(2)}, u32[]{:S(2)}) %collective-permute-start.9) | collective-permute-done | bytes 2097184 | tf_op jit(solution)/shard_map/ppermute | solution.py:251
  200.9 11.1 %collective-permute-done.12 = f32[384,512]{1,0:T(8,128)} collective-permute-done((f32[384,512]{1,0:T(8,128)}, f32[384,512]{1,0:T(8,128)}, u32[]{:S(2)}, u32[]{:S(2)}) %collective-permute-start.12) | collective-permute-done | bytes 786464 | tf_op jit(solution)/shard_map/ppermute | solution.py:19
  212.1 2.9 select_add_fusion.3
  218.0 5.4 %select_add_fusion.1 = f32[2,512,512]{2,1,0:T(8,128)} fusion(f32[2,512,512]{2,1,0:T(8,128)} %collective-permute-done.9, f32[2,512,512]{2,1,0:T(8,128)} %collective-permute-done.8, f32[2,512,512]{2,1,0:T(8,128)} %collective-permute-done.7, f32[2,512,512]{2,1,0:T(8,128)S(1)} %get-tuple-element.4, pred[512,512]{1,0:T(8,128)(4,1)S(1)} %copy-done.14, ...), kind=kLoop, calls=%fused_computation.7 | loop fusion | flops 3670016 | bytes 11534336 | tf_op jit(solution)/shard_map/add | solution.py:257
  224.8 2.4 collective-permute-start.13
  228.5 4.0 %collective-permute-start.22 = (f32[96,512]{1,0:T(8,128)S(1)}, f32[96,512]{1,0:T(8,128)S(1)}, u32[]{:S(2)}, u32[]{:S(2)}) collective-permute-start(f32[96,512]{1,0:T(8,128)S(1)} %slice_select_fusion.6), channel_id=1, source_target_pairs={{0,16},{8,24},{16,0},{24,8},{1,17},{9,25},{17,1},{25,9},{2,18},{10... | collective-permute-start | bytes 589832 | tf_op jit(solution)/shard_map/ppermute | solution.py:19
  232.5 2.7 collective-permute-done.13
  235.3 3.7 %collective-permute-start.14 = (f32[96,512]{1,0:T(8,128)S(1)}, f32[96,512]{1,0:T(8,128)S(1)}, u32[]{:S(2)}, u32[]{:S(2)}) collective-permute-start(f32[96,512]{1,0:T(8,128)S(1)} %slice_select_fusion.7), channel_id=1, source_target_pairs={{0,16},{8,24},{16,0},{24,8},{1,17},{9,25},{17,1},{25,9},{2,18},{10... | collective-permute-start | bytes 589832 | tf_op jit(solution)/shard_map/ppermute | solution.py:19
  239.0 45.8 %collective-permute-done.22 = f32[96,512]{1,0:T(8,128)S(1)} collective-permute-done((f32[96,512]{1,0:T(8,128)S(1)}, f32[96,512]{1,0:T(8,128)S(1)}, u32[]{:S(2)}, u32[]{:S(2)}) %collective-permute-start.22) | collective-permute-done | bytes 196640 | tf_op jit(solution)/shard_map/ppermute | solution.py:19
  285.0 4.4 %collective-permute-done.14 = f32[96,512]{1,0:T(8,128)S(1)} collective-permute-done((f32[96,512]{1,0:T(8,128)S(1)}, f32[96,512]{1,0:T(8,128)S(1)}, u32[]{:S(2)}, u32[]{:S(2)}) %collective-permute-start.14) | collective-permute-done | bytes 196640 | tf_op jit(solution)/shard_map/ppermute | solution.py:19
  289.5 3.1 collective-permute-done.23
  294.4 2.9 collective-permute-done.24
  299.8 13.4 %collective-permute-done.25 = f32[96,512]{1,0:T(8,128)S(1)} collective-permute-done((f32[96,512]{1,0:T(8,128)S(1)}, f32[96,512]{1,0:T(8,128)S(1)}, u32[]{:S(2)}, u32[]{:S(2)}) %collective-permute-start.25) | collective-permute-done | bytes 196640 | tf_op jit(solution)/shard_map/ppermute | solution.py:19
  314.4 3.0 collective-permute-done.17
  325.1 2.8 collective-permute-start.27
  331.0 15.5 %collective-permute-done.27 = f32[384,512]{1,0:T(8,128)S(1)} collective-permute-done((f32[384,512]{1,0:T(8,128)S(1)}, f32[384,512]{1,0:T(8,128)S(1)}, u32[]{:S(2)}, u32[]{:S(2)}) %collective-permute-start.27) | collective-permute-done | bytes 786464 | tf_op jit(solution)/shard_map/ppermute | solution.py:19
  349.0 2.6 collective-permute-start.28
  351.6 3.7 %add_add_fusion = (f32[2,512,512]{2,1,0:T(8,128)S(1)}, f32[2,512,512]{2,1,0:T(8,128)S(1)}) fusion(f32[2,512,512]{2,1,0:T(8,128)S(1)} %copy-done.4, f32[2,512,512]{2,1,0:T(8,128)} %collective-permute-done.9, f32[2,512,512]{2,1,0:T(8,128)} %collective-permute-done.8, f32[2,512,512]{2,1,0:T(8,128)} %collective-permute-done.7, ...), kind=kLoop, calls=%fused_computation.8 | loop fusion | flops 7864320 | bytes 16777216 | tf_op jit(solution)/shard_map/add | solution.py:285
  355.4 2.5 pad_maximum_fusion.1
  358.9 3.4 pad_maximum_fusion
  (132 shorter events, 56.2 us)
Async XLA Ops:
  3.7 46.7 %collective-permute-start.1 = (f32[2,512,512]{2,1,0:T(8,128)}, f32[2,512,512]{2,1,0:T(8,128)S(1)}, u32[]{:S(2)}, u32[]{:S(2)}) collective-permute-start(f32[2,512,512]{2,1,0:T(8,128)} %slice.170), channel_id=1, source_target_pairs={{8,0},{16,8},{24,16},{9,1},{17,9},{25,17},{10,2},{18,10},{26,18},{... | collective-permute-start | bytes 6291464 | tf_op jit(solution)/shard_map/ppermute | solution.py:25
  7.4 2.3 collective-permute-start
  16.1 0.7 collective-permute-start.3
  55.2 28.6 %collective-permute-start.5 = (f32[2,512,512]{2,1,0:T(8,128)}, f32[2,512,512]{2,1,0:T(8,128)}, u32[]{:S(2)}, u32[]{:S(2)}) collective-permute-start(f32[2,512,512]{2,1,0:T(8,128)} %get-tuple-element.12), channel_id=1, source_target_pairs={{2,1},{4,3},{6,5},{10,9},{12,11},{14,13},{18,17},{20,19},{22,21},{... | collective-permute-start | bytes 6291464 | tf_op jit(solution)/shard_map/ppermute | solution.py:224
  56.5 27.3 %collective-permute-start.4 = (f32[2,512,512]{2,1,0:T(8,128)}, f32[2,512,512]{2,1,0:T(8,128)}, u32[]{:S(2)}, u32[]{:S(2)}) collective-permute-start(f32[2,512,512]{2,1,0:T(8,128)} %get-tuple-element.13), channel_id=1, source_target_pairs={{2,0},{4,2},{6,4},{10,8},{12,10},{14,12},{18,16},{20,18},{22,20},{... | collective-permute-start | bytes 6291464 | tf_op jit(solution)/shard_map/ppermute | solution.py:223
  58.5 25.2 %collective-permute-start.2 = (f32[2,512,512]{2,1,0:T(8,128)}, f32[2,512,512]{2,1,0:T(8,128)}, u32[]{:S(2)}, u32[]{:S(2)}) collective-permute-start(f32[2,512,512]{2,1,0:T(8,128)} %get-tuple-element.14), channel_id=1, source_target_pairs={{0,1},{1,0},{2,3},{3,2},{4,5},{5,4},{6,7},{7,6},{8,9},{9,8},{10,11... | collective-permute-start | bytes 6291464 | tf_op jit(solution)/shard_map/ppermute | solution.py:19
  62.4 4.5 %collective-permute-start.6 = (f32[512,512]{1,0:T(8,128)}, f32[512,512]{1,0:T(8,128)S(1)}, u32[]{:S(2)}, u32[]{:S(2)}) collective-permute-start(f32[512,512]{1,0:T(8,128)} %slice_bitcast_fusion), channel_id=1, source_target_pairs={{0,1},{1,0},{2,3},{3,2},{4,5},{5,4},{6,7},{7,6},{8,9},{9,8},{10,11... | collective-permute-start | bytes 3145736 | tf_op jit(solution)/shard_map/ppermute | solution.py:19
  123.4 34.4 %collective-permute-start.11 = (f32[1536,512]{1,0:T(8,128)}, f32[1536,512]{1,0:T(8,128)}, u32[]{:S(2)}, u32[]{:S(2)}) collective-permute-start(f32[1536,512]{1,0:T(8,128)} %bitcast.31), channel_id=1, source_target_pairs={{0,1},{1,0},{2,3},{3,2},{4,5},{5,4},{6,7},{7,6},{8,9},{9,8},{10,11... | collective-permute-start | bytes 9437192 | tf_op jit(solution)/shard_map/ppermute | solution.py:19
  147.6 45.9 %collective-permute-start.9 = (f32[2,512,512]{2,1,0:T(8,128)S(1)}, f32[2,512,512]{2,1,0:T(8,128)}, u32[]{:S(2)}, u32[]{:S(2)}) collective-permute-start(f32[2,512,512]{2,1,0:T(8,128)S(1)} %get-tuple-element.4), channel_id=1, source_target_pairs={{1,2},{3,4},{5,6},{9,10},{11,12},{13,14},{17,18},{19,20},{21,22},{... | collective-permute-start | bytes 6291464 | tf_op jit(solution)/shard_map/ppermute | solution.py:251
  151.4 44.6 %collective-permute-start.8 = (f32[2,512,512]{2,1,0:T(8,128)S(1)}, f32[2,512,512]{2,1,0:T(8,128)}, u32[]{:S(2)}, u32[]{:S(2)}) collective-permute-start(f32[2,512,512]{2,1,0:T(8,128)S(1)} %get-tuple-element.4), channel_id=1, source_target_pairs={{0,2},{2,4},{4,6},{8,10},{10,12},{12,14},{16,18},{18,20},{20,22},{... | collective-permute-start | bytes 6291464 | tf_op jit(solution)/shard_map/ppermute | solution.py:250
  153.4 45.0 %collective-permute-start.7 = (f32[2,512,512]{2,1,0:T(8,128)S(1)}, f32[2,512,512]{2,1,0:T(8,128)}, u32[]{:S(2)}, u32[]{:S(2)}) collective-permute-start(f32[2,512,512]{2,1,0:T(8,128)S(1)} %get-tuple-element.4), channel_id=1, source_target_pairs={{0,1},{1,0},{2,3},{3,2},{4,5},{5,4},{6,7},{7,6},{8,9},{9,8},{10,11... | collective-permute-start | bytes 6291464 | tf_op jit(solution)/shard_map/ppermute | solution.py:19
  163.4 48.7 %collective-permute-start.12 = (f32[384,512]{1,0:T(8,128)}, f32[384,512]{1,0:T(8,128)}, u32[]{:S(2)}, u32[]{:S(2)}) collective-permute-start(f32[384,512]{1,0:T(8,128)} %get-tuple-element.17), channel_id=1, source_target_pairs={{0,2},{1,3},{2,0},{3,1},{4,6},{5,7},{6,4},{7,5},{8,10},{9,11},{10,... | collective-permute-start | bytes 2359304 | tf_op jit(solution)/shard_map/ppermute | solution.py:19
  164.2 47.9 %collective-permute-start.20 = (f32[384,512]{1,0:T(8,128)S(1)}, f32[384,512]{1,0:T(8,128)}, u32[]{:S(2)}, u32[]{:S(2)}) collective-permute-start(f32[384,512]{1,0:T(8,128)S(1)} %get-tuple-element.18), channel_id=1, source_target_pairs={{0,4},{1,5},{2,6},{3,7},{4,0},{5,1},{6,2},{7,3},{8,12},{9,13},{10,... | collective-permute-start | bytes 2359304 | tf_op jit(solution)/shard_map/ppermute | solution.py:19
  200.9 17.1 %copy-start.11 = (pred[512,512]{1,0:T(8,128)(4,1)S(1)}, pred[512,512]{1,0:T(8,128)(4,1)}, u32[]{:S(2)}) copy-start(pred[512,512]{1,0:T(8,128)(4,1)} %get-tuple-element.45) | copy-start | bytes 786436
  200.9 17.1 %copy-start.12 = (pred[512,512]{1,0:T(8,128)(4,1)S(1)}, pred[512,512]{1,0:T(8,128)(4,1)}, u32[]{:S(2)}) copy-start(pred[512,512]{1,0:T(8,128)(4,1)} %get-tuple-element.42) | copy-start | bytes 786436
  200.9 17.1 %copy-start.13 = (pred[512,512]{1,0:T(8,128)(4,1)S(1)}, pred[512,512]{1,0:T(8,128)(4,1)}, u32[]{:S(2)}) copy-start(pred[512,512]{1,0:T(8,128)(4,1)} %get-tuple-element.48) | copy-start | bytes 786436
  216.7 10.5 %collective-permute-start.21 = (f32[192,512]{1,0:T(8,128)}, f32[192,512]{1,0:T(8,128)}, u32[]{:S(2)}, u32[]{:S(2)}) collective-permute-start(f32[192,512]{1,0:T(8,128)} %slice_select_fusion.4), channel_id=1, source_target_pairs={{0,2},{1,3},{2,0},{3,1},{4,6},{5,7},{6,4},{7,5},{8,10},{9,11},{10,... | collective-permute-start | bytes 1179656 | tf_op jit(solution)/shard_map/ppermute | solution.py:19
  223.4 97.0 %collective-permute-start.10 = (f32[2,512,512]{2,1,0:T(8,128)}, f32[2,512,512]{2,1,0:T(8,128)S(1)}, u32[]{:S(2)}, u32[]{:S(2)}) collective-permute-start(f32[2,512,512]{2,1,0:T(8,128)} %select_add_fusion.1), channel_id=1, source_target_pairs={{0,8},{8,16},{16,24},{1,9},{9,17},{17,25},{2,10},{10,18},{18,26},{... | collective-permute-start | bytes 6291464 | tf_op jit(solution)/shard_map/ppermute | solution.py:25
  224.8 10.4 %collective-permute-start.13 = (f32[192,512]{1,0:T(8,128)S(1)}, f32[192,512]{1,0:T(8,128)S(1)}, u32[]{:S(2)}, u32[]{:S(2)}) collective-permute-start(f32[192,512]{1,0:T(8,128)S(1)} %slice_select_fusion.5), channel_id=1, source_target_pairs={{0,4},{1,5},{2,6},{3,7},{4,0},{5,1},{6,2},{7,3},{8,12},{9,13},{10,... | collective-permute-start | bytes 1179656 | tf_op jit(solution)/shard_map/ppermute | solution.py:19
  228.5 56.3 %collective-permute-start.22 = (f32[96,512]{1,0:T(8,128)S(1)}, f32[96,512]{1,0:T(8,128)S(1)}, u32[]{:S(2)}, u32[]{:S(2)}) collective-permute-start(f32[96,512]{1,0:T(8,128)S(1)} %slice_select_fusion.6), channel_id=1, source_target_pairs={{0,16},{8,24},{16,0},{24,8},{1,17},{9,25},{17,1},{25,9},{2,18},{10... | collective-permute-start | bytes 589832 | tf_op jit(solution)/shard_map/ppermute | solution.py:19
  235.3 54.0 %collective-permute-start.14 = (f32[96,512]{1,0:T(8,128)S(1)}, f32[96,512]{1,0:T(8,128)S(1)}, u32[]{:S(2)}, u32[]{:S(2)}) collective-permute-start(f32[96,512]{1,0:T(8,128)S(1)} %slice_select_fusion.7), channel_id=1, source_target_pairs={{0,16},{8,24},{16,0},{24,8},{1,17},{9,25},{17,1},{25,9},{2,18},{10... | collective-permute-start | bytes 589832 | tf_op jit(solution)/shard_map/ppermute | solution.py:19
  284.9 7.7 %collective-permute-start.23 = (f32[48,512]{1,0:T(8,128)S(1)}, f32[48,512]{1,0:T(8,128)S(1)}, u32[]{:S(2)}, u32[]{:S(2)}) collective-permute-start(f32[48,512]{1,0:T(8,128)S(1)} %slice_select_fusion.8), channel_id=1, source_target_pairs={{0,8},{8,0},{16,24},{24,16},{1,9},{9,1},{17,25},{25,17},{2,10},{10... | collective-permute-start | bytes 294920 | tf_op jit(solution)/shard_map/ppermute | solution.py:19
  289.5 4.8 %collective-permute-start.15 = (f32[48,512]{1,0:T(8,128)S(1)}, f32[48,512]{1,0:T(8,128)S(1)}, u32[]{:S(2)}, u32[]{:S(2)}) collective-permute-start(f32[48,512]{1,0:T(8,128)S(1)} %slice_select_fusion.9), channel_id=1, source_target_pairs={{0,8},{8,0},{16,24},{24,16},{1,9},{9,1},{17,25},{25,17},{2,10},{10... | collective-permute-start | bytes 294920 | tf_op jit(solution)/shard_map/ppermute | solution.py:19
  292.6 4.6 %collective-permute-start.24 = (f32[48,512]{1,0:T(8,128)S(1)}, f32[48,512]{1,0:T(8,128)S(1)}, u32[]{:S(2)}, u32[]{:S(2)}) collective-permute-start(f32[48,512]{1,0:T(8,128)S(1)} %select_add_fusion.8), channel_id=1, source_target_pairs={{0,8},{8,0},{16,24},{24,16},{1,9},{9,1},{17,25},{25,17},{2,10},{10... | collective-permute-start | bytes 294920 | tf_op jit(solution)/shard_map/ppermute | solution.py:19
  294.3 3.9 %collective-permute-start.16 = (f32[48,512]{1,0:T(8,128)S(1)}, f32[48,512]{1,0:T(8,128)S(1)}, u32[]{:S(2)}, u32[]{:S(2)}) collective-permute-start(f32[48,512]{1,0:T(8,128)S(1)} %select_add_fusion.9), channel_id=1, source_target_pairs={{0,8},{8,0},{16,24},{24,16},{1,9},{9,1},{17,25},{25,17},{2,10},{10... | collective-permute-start | bytes 294920 | tf_op jit(solution)/shard_map/ppermute | solution.py:19
  297.3 15.9 %collective-permute-start.25 = (f32[96,512]{1,0:T(8,128)S(1)}, f32[96,512]{1,0:T(8,128)S(1)}, u32[]{:S(2)}, u32[]{:S(2)}) collective-permute-start(f32[96,512]{1,0:T(8,128)S(1)} %pad_maximum_fusion.8), channel_id=1, source_target_pairs={{0,16},{8,24},{16,0},{24,8},{1,17},{9,25},{17,1},{25,9},{2,18},{10... | collective-permute-start | bytes 589832 | tf_op jit(solution)/shard_map/ppermute | solution.py:19
  298.3 19.2 %collective-permute-start.17 = (f32[96,512]{1,0:T(8,128)S(1)}, f32[96,512]{1,0:T(8,128)S(1)}, u32[]{:S(2)}, u32[]{:S(2)}) collective-permute-start(f32[96,512]{1,0:T(8,128)S(1)} %pad_maximum_fusion.7), channel_id=1, source_target_pairs={{0,16},{8,24},{16,0},{24,8},{1,17},{9,25},{17,1},{25,9},{2,18},{10... | collective-permute-start | bytes 589832 | tf_op jit(solution)/shard_map/ppermute | solution.py:19
  314.1 9.9 %collective-permute-start.26 = (f32[192,512]{1,0:T(8,128)}, f32[192,512]{1,0:T(8,128)}, u32[]{:S(2)}, u32[]{:S(2)}) collective-permute-start(f32[192,512]{1,0:T(8,128)} %pad_maximum_fusion.6), channel_id=1, source_target_pairs={{0,2},{1,3},{2,0},{3,1},{4,6},{5,7},{6,4},{7,5},{8,10},{9,11},{10,... | collective-permute-start | bytes 1179656 | tf_op jit(solution)/shard_map/ppermute | solution.py:19
  318.3 11.6 %collective-permute-start.18 = (f32[192,512]{1,0:T(8,128)}, f32[192,512]{1,0:T(8,128)}, u32[]{:S(2)}, u32[]{:S(2)}) collective-permute-start(f32[192,512]{1,0:T(8,128)} %pad_maximum_fusion.5), channel_id=1, source_target_pairs={{0,4},{1,5},{2,6},{3,7},{4,0},{5,1},{6,2},{7,3},{8,12},{9,13},{10,... | collective-permute-start | bytes 1179656 | tf_op jit(solution)/shard_map/ppermute | solution.py:19
  325.1 21.5 %collective-permute-start.27 = (f32[384,512]{1,0:T(8,128)S(1)}, f32[384,512]{1,0:T(8,128)S(1)}, u32[]{:S(2)}, u32[]{:S(2)}) collective-permute-start(f32[384,512]{1,0:T(8,128)S(1)} %pad_maximum_fusion.4), channel_id=1, source_target_pairs={{0,4},{1,5},{2,6},{3,7},{4,0},{5,1},{6,2},{7,3},{8,12},{9,13},{10,... | collective-permute-start | bytes 2359304 | tf_op jit(solution)/shard_map/ppermute | solution.py:19
  331.0 17.5 %collective-permute-start.19 = (f32[384,512]{1,0:T(8,128)S(1)}, f32[384,512]{1,0:T(8,128)S(1)}, u32[]{:S(2)}, u32[]{:S(2)}) collective-permute-start(f32[384,512]{1,0:T(8,128)S(1)} %pad_maximum_fusion.3), channel_id=1, source_target_pairs={{0,2},{1,3},{2,0},{3,1},{4,6},{5,7},{6,4},{7,5},{8,10},{9,11},{10,... | collective-permute-start | bytes 2359304 | tf_op jit(solution)/shard_map/ppermute | solution.py:19
  349.0 8.8 %collective-permute-start.28 = (f32[1536,512]{1,0:T(8,128)S(1)}, f32[1536,512]{1,0:T(8,128)S(1)}, u32[]{:S(2)}, u32[]{:S(2)}) collective-permute-start(f32[1536,512]{1,0:T(8,128)S(1)} %pad_maximum_fusion.2), channel_id=1, source_target_pairs={{0,1},{1,0},{2,3},{3,2},{4,5},{5,4},{6,7},{7,6},{8,9},{9,8},{10,11... | collective-permute-start | bytes 9437192 | tf_op jit(solution)/shard_map/ppermute | solution.py:19
  (14 other events, 63.9 us)
